TPU v7x, 32 devices: a whole 2x2x4 slice. The times are simulated.
32 devices in a mesh: dp: 2 (over y), expert: 16 (over z, x, core).
Axes of the slice: x: 2, y: 2, z: 4, core: 2. Of those that a mesh axis runs over, the one named last changes fastest.
Arguments:
- tokens: bfloat16 [1024, 2048], P(('dp', 'expert')), may hold values from -6 to 6
- routes: int32 [1024, 8], P(('dp', 'expert')), may hold values from 0 to 15, all different within a row; in each aligned block of 32 rows (0 to 31, 32 to 63, ...) at most 32 rows name the same one
- cotangent: bfloat16 [1024, 2048], P(('dp', 'expert')), may hold values from -6 to 6
- router_weight: bfloat16 [2048, 16], replicated, may hold values from -0.375 to 0.375
- gate_weight: bfloat16 [16, 2048, 768], P('expert'), may hold values from -0.125 to 0.125
- up_weight: bfloat16 [16, 2048, 768], P('expert'), may hold values from -0.125 to 0.125
- down_weight: bfloat16 [16, 768, 2048], P('expert'), may hold values from -0.21875 to 0.21875
Outputs:
- layer_out: bfloat16 [1024, 2048], P(('dp', 'expert'))
- token_grad: bfloat16 [1024, 2048], P(('dp', 'expert'))
- gate_grad: bfloat16 [16, 2048, 768], P('expert', 'dp')
- up_grad: bfloat16 [16, 2048, 768], P('expert', 'dp')
- down_grad: bfloat16 [16, 768, 2048], P('expert', None, 'dp')
- router_grad: float32 [2048, 16], replicated
Inputs may be any that keep to these rules, and one draw needn't show every extreme that they name: `routes`: each row names 8 different experts. Among the 32 rows of one device no expert is named by more than 32 rows, and in some device's rows an expert is named by exactly 32 rows.
All inputs are finite; a program needn't handle non-finite values.
Results may differ from a plain program's by a relative error of at most 0.0061.
Values may be sent and summed in bfloat16 or wider, within the bound.
A program may use at most 128 MiB of HBM per device.

v0:
```python
import jax
import jax.numpy as jnp
from jax import lax
from jax.sharding import PartitionSpec as P


def silu_parts(gate_act):
    sigmoid_value = jax.nn.sigmoid(gate_act)
    act_value = gate_act * sigmoid_value
    act_slope = sigmoid_value * (1.0 + gate_act * (1.0 - sigmoid_value))
    return (act_value, act_slope)


def expert_forward(arrived, gate_weight, up_weight, down_weight):
    gate_act = jnp.einsum(
        "sjcd,jdf->sjcf", arrived, gate_weight, preferred_element_type=jnp.float32
    )
    up_act = jnp.einsum("sjcd,jdf->sjcf", arrived, up_weight, preferred_element_type=jnp.float32)
    act_value, act_slope = silu_parts(gate_act)
    hidden = (act_value * up_act).astype(jnp.bfloat16)
    expert_out = jnp.einsum(
        "sjcf,jfd->sjcd", hidden, down_weight, preferred_element_type=jnp.float32
    ).astype(jnp.bfloat16)
    return (expert_out, (up_act, act_value, act_slope, hidden))


def expert_backward(arrived_grads, stored, gate_weight, up_weight, down_weight):
    up_act, act_value, act_slope, hidden = stored
    hidden_grad = jnp.einsum(
        "sjcd,jfd->sjcf", arrived_grads, down_weight, preferred_element_type=jnp.float32
    )
    gate_part = (hidden_grad * up_act * act_slope).astype(jnp.bfloat16)
    up_part = (hidden_grad * act_value).astype(jnp.bfloat16)
    input_grad = (
        jnp.einsum("sjcf,jdf->sjcd", gate_part, gate_weight, preferred_element_type=jnp.float32)
        + jnp.einsum("sjcf,jdf->sjcd", up_part, up_weight, preferred_element_type=jnp.float32)
    ).astype(jnp.bfloat16)
    return (input_grad, gate_part, up_part)


def local(tokens, routes, cotangent, router_weight, gate_weight, up_weight, down_weight):
    tok_rows, top_count = routes.shape
    model_width = tokens.shape[1]
    expert_count = router_weight.shape[1]
    local_count = gate_weight.shape[0]
    group_size = lax.axis_size("expert")
    capacity = min(tok_rows, 2 * tok_rows * top_count // expert_count)
    slot_total = expert_count * capacity
    buffer_shape = (group_size, local_count, capacity, model_width)
    logits = jnp.dot(tokens, router_weight, preferred_element_type=jnp.float32)
    exp_logits = jnp.exp(logits)
    probability = exp_logits / jnp.sum(exp_logits, axis=1, keepdims=True)
    chosen = (
        routes[:, :, None] == jnp.arange(expert_count, dtype=jnp.int32)[None, None, :]
    ).astype(jnp.int32)
    chosen_float = chosen.astype(jnp.float32)
    selected = jnp.sum(chosen_float * probability[:, None, :], axis=2)
    sel_total = jnp.sum(selected, axis=1, keepdims=True)
    combine = selected / sel_total
    per_token = jnp.sum(chosen, axis=1)
    earlier = jnp.cumsum(per_token, axis=0) - per_token
    slot_ids = jnp.sum(chosen * earlier[:, None, :], axis=2)
    flat_slot = routes * capacity + slot_ids
    match_map = (
        flat_slot[:, :, None] == jnp.arange(slot_total, dtype=jnp.int32)[None, None, :]
    ).astype(jnp.float32)
    presence = jnp.sum(match_map, axis=1)
    weight_map = jnp.sum(match_map * combine[:, :, None], axis=1)
    send_rows = (
        jnp.einsum(
            "tr,td->rd", presence.astype(jnp.bfloat16), tokens, preferred_element_type=jnp.float32
        )
        .astype(jnp.bfloat16)
        .reshape(buffer_shape)
    )
    send_grads = (
        jnp.einsum(
            "tr,td->rd", weight_map, cotangent.astype(jnp.float32), precision=lax.Precision.HIGHEST
        )
        .astype(jnp.bfloat16)
        .reshape(buffer_shape)
    )
    arrived = lax.all_to_all(send_rows, "expert", split_axis=0, concat_axis=0, tiled=True)
    expert_out, stored = expert_forward(arrived, gate_weight, up_weight, down_weight)
    returned = lax.all_to_all(expert_out, "expert", split_axis=0, concat_axis=0, tiled=True)
    arrived_grads = lax.all_to_all(send_grads, "expert", split_axis=0, concat_axis=0, tiled=True)
    input_grad, gate_part, up_part = expert_backward(
        arrived_grads, stored, gate_weight, up_weight, down_weight
    )
    returned_grads = lax.all_to_all(input_grad, "expert", split_axis=0, concat_axis=0, tiled=True)
    hidden = stored[3]
    gate_term = jnp.einsum("sjcd,sjcf->jdf", arrived, gate_part, preferred_element_type=jnp.float32)
    up_term = jnp.einsum("sjcd,sjcf->jdf", arrived, up_part, preferred_element_type=jnp.float32)
    down_term = jnp.einsum(
        "sjcf,sjcd->jfd", hidden, arrived_grads, preferred_element_type=jnp.float32
    )
    gate_sum, up_sum, down_sum = (
        lax.psum_scatter(gate_term, "dp", scatter_dimension=1, tiled=True),
        lax.psum_scatter(up_term, "dp", scatter_dimension=1, tiled=True),
        lax.psum_scatter(down_term, "dp", scatter_dimension=2, tiled=True),
    )
    gate_grad = gate_sum.astype(jnp.bfloat16)
    up_grad = up_sum.astype(jnp.bfloat16)
    down_grad = down_sum.astype(jnp.bfloat16)
    flat_index = flat_slot.reshape(-1)
    out_sel = jnp.take(returned.reshape(slot_total, model_width), flat_index, axis=0).reshape(
        tok_rows, top_count, model_width
    )
    grad_sel = jnp.take(
        returned_grads.reshape(slot_total, model_width), flat_index, axis=0
    ).reshape(tok_rows, top_count, model_width)
    layer_out = jnp.sum(combine[:, :, None] * out_sel.astype(jnp.float32), axis=1).astype(
        jnp.bfloat16
    )
    comb_grad = jnp.einsum("tkd,td->tk", out_sel, cotangent, preferred_element_type=jnp.float32)
    sel_grad = (comb_grad - jnp.sum(combine * comb_grad, axis=1, keepdims=True)) / sel_total
    prob_grad = jnp.sum(chosen_float * sel_grad[:, :, None], axis=1)
    logit_grad = probability * (prob_grad - jnp.sum(probability * prob_grad, axis=1, keepdims=True))
    router_term = jnp.einsum(
        "td,te->de", tokens.astype(jnp.float32), logit_grad, precision=lax.Precision.HIGHEST
    )
    router_grad = lax.psum(router_term, ("dp", "expert"))
    router_back = jnp.einsum(
        "te,de->td", logit_grad, router_weight.astype(jnp.float32), precision=lax.Precision.HIGHEST
    )
    token_grad = (jnp.sum(grad_sel.astype(jnp.float32), axis=1) + router_back).astype(jnp.bfloat16)
    return (layer_out, token_grad, gate_grad, up_grad, down_grad, router_grad)


def solution(mesh):
    return jax.shard_map(
        local,
        mesh=mesh,
        in_specs=(
            P(("dp", "expert"), None),
            P(("dp", "expert"), None),
            P(("dp", "expert"), None),
            P(),
            P("expert", None, None),
            P("expert", None, None),
            P("expert", None, None),
        ),
        out_specs=(
            P(("dp", "expert"), None),
            P(("dp", "expert"), None),
            P("expert", "dp", None),
            P("expert", "dp", None),
            P("expert", None, "dp"),
            P(),
        ),
        check_vma=False,
    )
```

profile of v0, /device:TPU:0, one launch (start us, length us, event | category | flops | bytes accessed | tf_op | source)
XLA Modules:
  0.0 455.1 jit_solution(14684139448227573478)
XLA Ops:
  8.0 0.9 convert_reduce_fusion.2
  8.9 0.1 copy.29
  8.9 1.1 fusion.55
  10.1 0.7 fusion.48
  10.8 0.1 copy.28
  10.9 0.1 reduce_window_sum.11
  10.9 0.1 copy.31
  11.0 0.7 select_reduce_fusion.1
  11.7 0.7 multiply_add_fusion
  12.4 0.1 copy.32
  12.5 0.4 select_reduce_fusion
  12.9 4.0 convolution_convert_fusion
  16.9 7.5 %all-to-all-start.2 = ((bf16[16,1,32,2048]{3,2,1,0:T(8,128)(2,1)}), bf16[16,1,32,2048]{3,2,1,0:T(8,128)(2,1)}, u32[]{:S(2)}, u32[]{:S(2)}) async-start(bf16[16,1,32,2048]{3,2,1,0:T(8,128)(2,1)} %bitcast.170), calls=%async_computation.2 | async-start | bytes 4194304 | tf_op jit(solution)/shard_map/all_to_all | solution.py:86
  24.5 2.1 convolution_convert_fusion.1
  26.6 39.1 %all-to-all-done.2 = bf16[16,1,32,2048]{3,2,1,0:T(8,128)(2,1)} async-done(((bf16[16,1,32,2048]{3,2,1,0:T(8,128)(2,1)}), bf16[16,1,32,2048]{3,2,1,0:T(8,128)(2,1)}, u32[]{:S(2)}, u32[]{:S(2)}) %all-to-all-start.2) | async-done | bytes 2097184 | tf_op jit(solution)/shard_map/all_to_all | solution.py:86
  65.7 11.3 %all-to-all-start = ((bf16[16,1,32,2048]{3,2,1,0:T(8,128)(2,1)}), bf16[16,1,32,2048]{3,2,1,0:T(8,128)(2,1)}, u32[]{:S(2)}, u32[]{:S(2)}) async-start(bf16[16,1,32,2048]{3,2,1,0:T(8,128)(2,1)} %bitcast.169), calls=%async_computation | async-start | bytes 4194304 | tf_op jit(solution)/shard_map/all_to_all | solution.py:83
  77.0 5.5 %fusion = f32[16,32,768]{2,1,0:T(8,128)} fusion(bf16[1,768,2048]{2,1,0:T(8,128)(2,1)} %param.15, bf16[16,1,32,2048]{3,2,1,0:T(8,128)(2,1)} %all-to-all-done.2), kind=kOutput, calls=%fused_computation.6 | convolution fusion | flops 1610612736 | bytes 6815744 | tf_op jit(solution)/shard_map/sjcd,jfd->sjcf/dot_general | solution.py:29
  82.5 35.6 %all-to-all-done = bf16[16,1,32,2048]{3,2,1,0:T(8,128)(2,1)} async-done(((bf16[16,1,32,2048]{3,2,1,0:T(8,128)(2,1)}), bf16[16,1,32,2048]{3,2,1,0:T(8,128)(2,1)}, u32[]{:S(2)}, u32[]{:S(2)}) %all-to-all-start) | async-done | bytes 2097184 | tf_op jit(solution)/shard_map/all_to_all | solution.py:83
  118.1 4.4 fusion.6
  122.5 5.1 %fusion.41 = (bf16[16,32,768]{2,1,0:T(8,128)(2,1)S(1)}, bf16[16,1,32,768]{3,2,0,1:T(8,128)(2,1)}, bf16[16,32,768]{2,1,0:T(8,128)(2,1)}) fusion(f32[16,32,768]{2,1,0:T(8,128)S(1)} %fusion.6, f32[16,32,768]{2,1,0:T(8,128)S(1)} %copy-done.6, bf16[1,2048,768]{2,1,0:T(8,128)(2,1)S(1)} %copy-done, bf16[16,1,32,2048]{3,2,1,0:T(8,128)(2,1)} %all-to-all-done), kind=kOutput, calls=%fused_computation.53 | convolution fusion | flops 1616510976 | bytes 10747904 | tf_op jit(solution)/shard_map/sjcd,jdf->sjcf/dot_general | solution.py:15
  127.6 0.9 copy-done.7
  128.5 6.1 %convolution_bitcast_fusion = f32[1,768,2048]{2,1,0:T(8,128)} fusion(bf16[16,32,768]{2,1,0:T(8,128)(2,1)S(1)} %get-tuple-element.13, bf16[16,1,32,2048]{3,2,1,0:T(8,128)(2,1)} %all-to-all-done.2), kind=kOutput, calls=%fused_computation.3 | convolution fusion | flops 1610612736 | bytes 9175040 | tf_op jit(solution)/shard_map/sjcf,sjcd->jfd/dot_general | solution.py:94
  134.7 6.3 %convolution_bitcast_fusion.2 = f32[1,2048,768]{2,1,0:T(8,128)} fusion(bf16[16,1,32,2048]{3,2,1,0:T(8,128)(2,1)} %all-to-all-done, bf16[16,1,32,768]{3,2,0,1:T(8,128)(2,1)} %get-tuple-element.14), kind=kOutput, calls=%fused_computation.5 | convolution fusion | flops 1610612736 | bytes 9175040 | tf_op jit(solution)/shard_map/sjcd,sjcf->jdf/dot_general | solution.py:92
  141.0 0.2 reduce-scatter.6.cloned.1.call-start
  141.2 6.3 %convolution_bitcast_fusion.1 = f32[1,2048,768]{2,1,0:T(8,128)} fusion(bf16[16,32,768]{2,1,0:T(8,128)(2,1)} %get-tuple-element.15, bf16[16,1,32,2048]{3,2,1,0:T(8,128)(2,1)} %all-to-all-done), kind=kOutput, calls=%fused_computation.4 | convolution fusion | flops 1610612736 | bytes 9175040 | tf_op jit(solution)/shard_map/sjcd,sjcf->jdf/dot_general | solution.py:93
  147.5 5.6 %fusion.17 = bf16[16,1,32,2048]{3,2,1,0:T(8,128)(2,1)} fusion(bf16[16,32,768]{2,1,0:T(8,128)(2,1)} %copy-done.7, bf16[1,768,2048]{2,1,0:T(8,128)(2,1)} %param.15), kind=kOutput, calls=%fused_computation.21 | convolution fusion | flops 1611661312 | bytes 6029312 | tf_op jit(solution)/shard_map/sjcf,jfd->sjcd/dot_general | solution.py:21
  153.1 11.6 %all-to-all-start.1 = ((bf16[16,1,32,2048]{3,2,1,0:T(8,128)(2,1)}), bf16[16,1,32,2048]{3,2,1,0:T(8,128)(2,1)}, u32[]{:S(2)}, u32[]{:S(2)}) async-start(bf16[16,1,32,2048]{3,2,1,0:T(8,128)(2,1)} %fusion.17), calls=%async_computation.1 | async-start | bytes 4194304 | tf_op jit(solution)/shard_map/all_to_all | solution.py:85
  164.8 4.0 fusion.4
  168.8 3.1 fusion.20
  171.9 34.0 %all-to-all-done.1 = bf16[16,1,32,2048]{3,2,1,0:T(8,128)(2,1)} async-done(((bf16[16,1,32,2048]{3,2,1,0:T(8,128)(2,1)}), bf16[16,1,32,2048]{3,2,1,0:T(8,128)(2,1)}, u32[]{:S(2)}, u32[]{:S(2)}) %all-to-all-start.1) | async-done | bytes 2097184 | tf_op jit(solution)/shard_map/all_to_all | solution.py:85
  205.9 11.3 %all-to-all-start.3 = ((bf16[16,1,32,2048]{3,2,1,0:T(8,128)(2,1)}), bf16[16,1,32,2048]{3,2,1,0:T(8,128)(2,1)}, u32[]{:S(2)}, u32[]{:S(2)}) async-start(bf16[16,1,32,2048]{3,2,1,0:T(8,128)(2,1)} %fusion.20), calls=%async_computation.3 | async-start | bytes 4194304 | tf_op jit(solution)/shard_map/all_to_all | solution.py:90
  217.2 0.0 all-reduce.2.cloned.1.call-start
  217.2 0.1 reshape.125
  217.4 5.3 %gather_fusion = bf16[256,2048]{1,0:T(8,128)(2,1)} fusion(bf16[512,2048]{1,0:T(8,128)(2,1)} %bitcast.22, s32[1024]{0:T(1024)S(1)} %pad_clamp_fusion), kind=kCustom, calls=%fused_computation.clone | custom fusion | bytes 2098176 | tf_op jit(solution)/shard_map/jit(_take)/gather | solution.py:106
  222.7 2.1 fusion.39
  224.8 0.1 copy.40
  224.9 33.4 %all-to-all-done.3 = bf16[16,1,32,2048]{3,2,1,0:T(8,128)(2,1)} async-done(((bf16[16,1,32,2048]{3,2,1,0:T(8,128)(2,1)}), bf16[16,1,32,2048]{3,2,1,0:T(8,128)(2,1)}, u32[]{:S(2)}, u32[]{:S(2)}) %all-to-all-start.3) | async-done | bytes 2097184 | tf_op jit(solution)/shard_map/all_to_all | solution.py:90
  258.3 5.2 %gather_fusion.1 = bf16[256,2048]{1,0:T(8,128)(2,1)} fusion(bf16[512,2048]{1,0:T(8,128)(2,1)} %bitcast.40, s32[1024]{0:T(1024)S(1)} %pad_clamp_fusion), kind=kCustom, calls=%fused_computation.1.clone | custom fusion | bytes 2098176 | tf_op jit(solution)/shard_map/jit(_take)/gather | solution.py:109
  263.6 0.9 convolution_bitcast_fusion.3
  264.5 4.0 convert_reduce_fusion
  268.5 1.0 fusion.23
  269.5 3.3 convert_element_type.102
  272.7 25.2 %reduce-scatter.4.cloned.1.call-done = f32[1,1024,768]{2,1,0:T(8,128)} async-done(((f32[1,2048,768]{2,1,0:T(8,128)}), f32[1,1024,768]{2,1,0:T(8,128)}) %reduce-scatter.4.cloned.1.call-update) | async-done | bytes 3145744 | tf_op jit(solution)/shard_map/reduce_scatter | solution.py:98
  297.9 3.2 convert_element_type.100
  301.1 76.4 %reduce-scatter.6.cloned.1.call-done = f32[1,1024,768]{2,1,0:T(8,128)} async-done(((f32[1,2048,768]{2,1,0:T(8,128)}), f32[1,1024,768]{2,1,0:T(8,128)}) %reduce-scatter.6.cloned.1.call-update) | async-done | bytes 3145744 | tf_op jit(solution)/shard_map/reduce_scatter | solution.py:99
  377.6 3.2 convert_element_type.101
  380.8 65.6 %all-reduce.2.cloned.1.call-done = f32[2048,16]{0,1:T(8,128)} async-done(((f32[2048,16]{0,1:T(8,128)}), f32[2048,16]{0,1:T(8,128)}) %all-reduce.2.cloned.1.call-update) | async-done | bytes 131088 | tf_op jit(solution)/shard_map/psum | solution.py:122
  446.4 1.6 copy.44
  (32 shorter events, 0.3 us)
Async XLA Ops:
  8.0 114.5 %copy-start = (bf16[1,2048,768]{2,1,0:T(8,128)(2,1)S(1)}, bf16[1,2048,768]{2,1,0:T(8,128)(2,1)}, u32[]{:S(2)}) copy-start(bf16[1,2048,768]{2,1,0:T(8,128)(2,1)} %param.13) | copy-start | bytes 9437188
  16.9 7.6 %copy-start.1 = (bf16[32,2048]{1,0:T(8,128)(2,1)S(1)}, bf16[32,2048]{1,0:T(8,128)(2,1)}, u32[]{:S(2)}) copy-start(bf16[32,2048]{1,0:T(8,128)(2,1)} %param.9) | copy-start | bytes 393220
  16.9 48.7 %all-to-all-start.2 = ((bf16[16,1,32,2048]{3,2,1,0:T(8,128)(2,1)}), bf16[16,1,32,2048]{3,2,1,0:T(8,128)(2,1)}, u32[]{:S(2)}, u32[]{:S(2)}) async-start(bf16[16,1,32,2048]{3,2,1,0:T(8,128)(2,1)} %bitcast.170), calls=%async_computation.2 | async-start | bytes 4194304 | tf_op jit(solution)/shard_map/all_to_all | solution.py:86
  65.7 52.4 %all-to-all-start = ((bf16[16,1,32,2048]{3,2,1,0:T(8,128)(2,1)}), bf16[16,1,32,2048]{3,2,1,0:T(8,128)(2,1)}, u32[]{:S(2)}, u32[]{:S(2)}) async-start(bf16[16,1,32,2048]{3,2,1,0:T(8,128)(2,1)} %bitcast.169), calls=%async_computation | async-start | bytes 4194304 | tf_op jit(solution)/shard_map/all_to_all | solution.py:83
  76.9 192.5 %reduce-scatter.8.cloned.1.call-start = ((), (), s32[]{:S(2)}) async-start(), calls=%async_computation.9 | async-start | bytes 9437184 | tf_op jit(solution)/shard_map/reduce_scatter | solution.py:100
  118.1 4.4 copy-start.6
  127.6 0.9 copy-start.7
  134.6 163.3 %reduce-scatter.4.cloned.1.call-start = ((), (), s32[]{:S(2)}) async-start(), calls=%async_computation.7 | async-start | bytes 9437184 | tf_op jit(solution)/shard_map/reduce_scatter | solution.py:98
  141.0 236.6 %reduce-scatter.6.cloned.1.call-start = ((), (), s32[]{:S(2)}) async-start(), calls=%async_computation.8 | async-start | bytes 9437184 | tf_op jit(solution)/shard_map/reduce_scatter | solution.py:99
  153.1 52.8 %all-to-all-start.1 = ((bf16[16,1,32,2048]{3,2,1,0:T(8,128)(2,1)}), bf16[16,1,32,2048]{3,2,1,0:T(8,128)(2,1)}, u32[]{:S(2)}, u32[]{:S(2)}) async-start(bf16[16,1,32,2048]{3,2,1,0:T(8,128)(2,1)} %fusion.17), calls=%async_computation.1 | async-start | bytes 4194304 | tf_op jit(solution)/shard_map/all_to_all | solution.py:85
  164.7 4.0 copy-start.5
  205.9 52.4 %all-to-all-start.3 = ((bf16[16,1,32,2048]{3,2,1,0:T(8,128)(2,1)}), bf16[16,1,32,2048]{3,2,1,0:T(8,128)(2,1)}, u32[]{:S(2)}, u32[]{:S(2)}) async-start(bf16[16,1,32,2048]{3,2,1,0:T(8,128)(2,1)} %fusion.20), calls=%async_computation.3 | async-start | bytes 4194304 | tf_op jit(solution)/shard_map/all_to_all | solution.py:90
  217.2 229.2 %all-reduce.2.cloned.1.call-start = ((), (), s32[]{:S(2)}) async-start(), calls=%async_computation.10 | async-start | bytes 262144 | tf_op jit(solution)/shard_map/psum | solution.py:122
  217.4 5.4 %copy-start.3 = (bf16[32,2048]{1,0:T(8,128)(2,1)S(1)}, bf16[32,2048]{1,0:T(8,128)(2,1)}, u32[]{:S(2)}) copy-start(bf16[32,2048]{1,0:T(8,128)(2,1)} %param.11) | copy-start | bytes 393220
  258.3 5.2 %copy-start.4 = (s32[32,8]{0,1:T(8,128)S(1)}, s32[32,8]{0,1:T(8,128)}, u32[]{:S(2)}) copy-start(s32[32,8]{0,1:T(8,128)} %param.10) | copy-start | bytes 3076
  263.5 4.9 %copy-start.2 = (bf16[2048,16]{0,1:T(8,128)(2,1)S(1)}, bf16[2048,16]{0,1:T(8,128)(2,1)}, u32[]{:S(2)}) copy-start(bf16[2048,16]{0,1:T(8,128)(2,1)} %param.12) | copy-start | bytes 196612
Sparse Core Ops, SparseCore 0:
  134.7 83.5 reduce-scatter.7
  220.8 77.0 reduce-scatter.3
  300.2 77.2 reduce-scatter.5
Sparse Core Ops, SparseCore 1:
  268.6 177.8 all-reduce.1
where the time goes:
time: 456 us; the launch traced here: 455 us
  waiting for transfers between devices  309 us (68%)
  matrix products  57.6 us (13%)
  starting transfers between devices  42 us (9%)
  other arithmetic  17.2 us (4%)
  between operations  15.4 us (3%)
  local copies, waits for them, and re-layouts  13.5 us (3%)
    reduce_scatter x1, waiting for transfers between devices, local(): lax.psum_scatter(up_term, 'dp', scatter_dimension=1, tiled=True)  76.4 us
    psum x1, waiting for transfers between devices, local(): router_grad = lax.psum(router_term, ('dp', 'expert'))  65.6 us
    all_to_all x1, waiting for transfers between devices, local(): lax.all_to_all(send_grads, 'expert', split_axis=0, concat_axis=0, tiled=T...  39.1 us
    all_to_all x1, waiting for transfers between devices, local(): lax.all_to_all(send_rows, 'expert', split_axis=0, concat_axis=0, tiled=True)  35.6 us
    all_to_all x1, waiting for transfers between devices, local(): lax.all_to_all(expert_out, 'expert', split_axis=0, concat_axis=0, tiled=T...  34 us
    all_to_all x1, waiting for transfers between devices, local(): lax.all_to_all(input_grad, 'expert', split_axis=0, concat_axis=0, tiled=T...  33.4 us
    reduce_scatter x1, waiting for transfers between devices, local(): lax.psum_scatter(gate_term, 'dp', scatter_dimension=1, tiled=True)  25.2 us
    all_to_all x1, starting transfers between devices, local(): lax.all_to_all(expert_out, 'expert', split_axis=0, concat_axis=0, tiled=T...  11.6 us
  transfers between devices with their start and end apart: 8, of which 7 were waited for; matrix products, arithmetic and copies ran while one was open for 13% of the time, Pallas kernels for 0%

commit v1 on v0

--- a/solution.py
+++ b/solution.py
@@ -38,7 +38,7 @@
     return (input_grad, gate_part, up_part)
 
 
-def local(tokens, routes, cotangent, router_weight, gate_weight, up_weight, down_weight):
+def local_slots(tokens, routes, cotangent, router_weight, gate_weight, up_weight, down_weight):
     tok_rows, top_count = routes.shape
     model_width = tokens.shape[1]
     expert_count = router_weight.shape[1]
@@ -58,7 +58,8 @@
     sel_total = jnp.sum(selected, axis=1, keepdims=True)
     combine = selected / sel_total
     per_token = jnp.sum(chosen, axis=1)
-    earlier = jnp.cumsum(per_token, axis=0) - per_token
+    before = jnp.tril(jnp.ones((tok_rows, tok_rows), jnp.float32), -1)
+    earlier = jnp.dot(before, per_token.astype(jnp.float32)).astype(jnp.int32)
     slot_ids = jnp.sum(chosen * earlier[:, None, :], axis=2)
     flat_slot = routes * capacity + slot_ids
     match_map = (
@@ -127,6 +128,111 @@
     return (layer_out, token_grad, gate_grad, up_grad, down_grad, router_grad)
 
 
+def local_dense(tokens, routes, cotangent, router_weight, gate_weight, up_weight, down_weight):
+    tok_rows = tokens.shape[0]
+    model_width = tokens.shape[1]
+    expert_count = router_weight.shape[1]
+    group_size = lax.axis_size("expert")
+    dp_size = lax.axis_size("dp")
+    dp_index = lax.axis_index("dp")
+    expert_index = lax.axis_index("expert")
+    both = ("dp", "expert")
+    gate_mat, up_mat, down_mat = gate_weight[0], up_weight[0], down_weight[0]
+    routes_all = lax.all_gather(routes, both, axis=0, tiled=True)
+    tokens_all = lax.all_gather(tokens, both, axis=0, tiled=True)
+    cot_all = lax.all_gather(cotangent, both, axis=0, tiled=True)
+    logits = jnp.dot(tokens_all, router_weight, preferred_element_type=jnp.float32)
+    exp_logits = jnp.exp(logits)
+    probability = exp_logits / jnp.sum(exp_logits, axis=1, keepdims=True)
+    chosen = jnp.sum(
+        (
+            routes_all[:, :, None] == jnp.arange(expert_count, dtype=jnp.int32)[None, None, :]
+        ).astype(jnp.float32),
+        axis=1,
+    )
+    selected = chosen * probability
+    sel_total = jnp.sum(selected, axis=1, keepdims=True)
+    combine = selected / sel_total
+    mine = (jnp.arange(expert_count, dtype=jnp.int32) == expert_index).astype(jnp.float32)
+    scale = jnp.sum(combine * mine[None, :], axis=1, keepdims=True)
+    gate_act = jnp.dot(tokens_all, gate_mat, preferred_element_type=jnp.float32)
+    up_act = jnp.dot(tokens_all, up_mat, preferred_element_type=jnp.float32)
+    raw_grad = lax.dot_general(
+        cot_all, down_mat, (((1,), (1,)), ((), ())), preferred_element_type=jnp.float32
+    )
+    act_value, act_slope = silu_parts(gate_act)
+    hidden = act_value * up_act
+    comb_mine = jnp.sum(hidden * raw_grad, axis=1)
+    scaled_hidden = (hidden * scale).astype(jnp.bfloat16)
+    hidden_grad = raw_grad * scale
+    gate_part = (hidden_grad * up_act * act_slope).astype(jnp.bfloat16)
+    up_part = (hidden_grad * act_value).astype(jnp.bfloat16)
+    group_rows = group_size * tok_rows
+    first = dp_index * group_rows
+
+    def rows_of(array):
+        return lax.dynamic_slice_in_dim(array, first, group_rows, axis=0)
+
+    out_term = jnp.dot(
+        rows_of(scaled_hidden), down_mat, preferred_element_type=jnp.float32
+    ).astype(jnp.bfloat16)
+    layer_out = lax.psum_scatter(out_term, "expert", scatter_dimension=0, tiled=True)
+    in_term = (
+        lax.dot_general(
+            rows_of(gate_part), gate_mat, (((1,), (1,)), ((), ())),
+            preferred_element_type=jnp.float32,
+        )
+        + lax.dot_general(
+            rows_of(up_part), up_mat, (((1,), (1,)), ((), ())),
+            preferred_element_type=jnp.float32,
+        )
+    ).astype(jnp.bfloat16)
+    in_sum = lax.psum_scatter(in_term, "expert", scatter_dimension=0, tiled=True)
+    part_width = model_width // dp_size
+    start = dp_index * part_width
+    tokens_part = lax.dynamic_slice_in_dim(tokens_all, start, part_width, axis=1)
+    cot_part = lax.dynamic_slice_in_dim(cot_all, start, part_width, axis=1)
+    over_rows = (((0,), (0,)), ((), ()))
+    gate_grad = lax.dot_general(
+        tokens_part, gate_part, over_rows, preferred_element_type=jnp.float32
+    ).astype(jnp.bfloat16)
+    up_grad = lax.dot_general(
+        tokens_part, up_part, over_rows, preferred_element_type=jnp.float32
+    ).astype(jnp.bfloat16)
+    down_grad = lax.dot_general(
+        scaled_hidden, cot_part, over_rows, preferred_element_type=jnp.float32
+    ).astype(jnp.bfloat16)
+    comb_grad = lax.all_gather(comb_mine, "expert", axis=0).T
+    sel_grad = (
+        chosen * (comb_grad - jnp.sum(combine * comb_grad, axis=1, keepdims=True)) / sel_total
+    )
+    logit_grad = probability * (sel_grad - jnp.sum(probability * sel_grad, axis=1, keepdims=True))
+    router_grad = jnp.einsum(
+        "td,te->de",
+        tokens_all.astype(jnp.float32),
+        logit_grad,
+        precision=lax.Precision.HIGHEST,
+    )
+    own_first = (dp_index * group_size + expert_index) * tok_rows
+    own_logit_grad = lax.dynamic_slice_in_dim(logit_grad, own_first, tok_rows, axis=0)
+    router_back = jnp.einsum(
+        "te,de->td",
+        own_logit_grad,
+        router_weight.astype(jnp.float32),
+        precision=lax.Precision.HIGHEST,
+    )
+    token_grad = (in_sum.astype(jnp.float32) + router_back).astype(jnp.bfloat16)
+    return (layer_out, token_grad, gate_grad[None], up_grad[None], down_grad[None], router_grad)
+
+
+def local(tokens, routes, cotangent, router_weight, gate_weight, up_weight, down_weight):
+    tok_rows, top_count = routes.shape
+    capacity = min(tok_rows, 2 * tok_rows * top_count // router_weight.shape[1])
+    dense = capacity == tok_rows and gate_weight.shape[0] == 1
+    plan = local_dense if dense else local_slots
+    return plan(tokens, routes, cotangent, router_weight, gate_weight, up_weight, down_weight)
+
+
 def solution(mesh):
     return jax.shard_map(
         local,

time: 456 us -> 313 us (0.69)
  waiting for transfers between devices: 309 us -> 175 us
  blocking collectives: 0 us -> 64.1 us
  starting transfers between devices: 42 us -> 0.38 us
  local copies, waits for them, and re-layouts: 13.5 us -> 1.34 us
  other arithmetic: 17.2 us -> 5.2 us
  matrix products: 57.6 us -> 52.5 us
    all_to_all x4 -> x0, waiting for transfers between devices: 142 us -> none  [the longest x1 39.1 us: local(): lax.all_to_all(send_grads, 'expert', split_axis=0, concat_axis=0, tiled=T...]
    all_gather x0 -> x2, waiting for transfers between devices: none -> 72.3 us  [the longest x1 49.6 us: local_dense(): cot_all = lax.all_gather(cotangent, both, axis=0, tiled=True)]
    psum x1 -> x0, waiting for transfers between devices: 65.6 us -> none  [local(): router_grad = lax.psum(router_term, ('dp', 'expert'))]
    all_gather x0 -> x2, blocking collectives: none -> 64.1 us  [the longest x1 44.1 us: local_dense(): routes_all = lax.all_gather(routes, both, axis=0, tiled=True)]
    all_to_all x4 -> x0, starting transfers between devices: 41.7 us -> none  [the longest x1 11.6 us: local(): lax.all_to_all(expert_out, 'expert', split_axis=0, concat_axis=0, tiled=T...]
    gather x2 -> x0, local copies, waits for them, and re-layouts: 10.5 us -> none  [the longest x1 5.34 us: local(): jnp.take(returned.reshape(slot_total, model_width), flat_index, axis=0)]
    reduce_sum x8 -> x4, other arithmetic: 6.73 us -> 0.2 us  [the longest x1 0.09 us: local_dense(): jnp.sum(combine * comb_grad, axis=1, keepdims=True)]
    dot_general x15 -> x12, matrix products: 57.6 us -> 52.5 us  [the longest x1 8.5 us: local_dense(): gate_act = jnp.dot(tokens_all, gate_mat, preferred_element_type=jnp.float32)]
  transfers between devices with their start and end apart: 8 -> 4, of which waited for: 7 -> 4; matrix products, arithmetic and copies ran while one was open for 13% -> 12% of each run, Pallas kernels for 0% -> 0%
where the time goes in v1:
time: 313 us; the launch traced here: 312 us
  waiting for transfers between devices  175 us (56%)
  blocking collectives  64.1 us (20%)
  matrix products  52.5 us (17%)
  between operations  13.9 us (4%)
  other arithmetic  5.2 us (2%)
    reduce_scatter x1, waiting for transfers between devices, local_dense(): lax.psum_scatter(out_term, 'expert', scatter_dimension=0, tiled=True)  63.3 us
    all_gather x1, waiting for transfers between devices, local_dense(): cot_all = lax.all_gather(cotangent, both, axis=0, tiled=True)  49.6 us
    all_gather x1, blocking collectives, local_dense(): routes_all = lax.all_gather(routes, both, axis=0, tiled=True)  44.1 us
    reduce_scatter x1, waiting for transfers between devices, local_dense(): lax.psum_scatter(in_term, 'expert', scatter_dimension=0, tiled=True)  38 us
    all_gather x1, waiting for transfers between devices, local_dense(): tokens_all = lax.all_gather(tokens, both, axis=0, tiled=True)  22.7 us
    all_gather x1, blocking collectives, local_dense(): comb_grad = lax.all_gather(comb_mine, 'expert', axis=0).T  20 us
    dot_general x1, matrix products, local_dense(): gate_act = jnp.dot(tokens_all, gate_mat, preferred_element_type=jnp.float32)  8.5 us
    dot_general x1, matrix products, local_dense(): lax.dot_general(cot_all, down_mat, (((1,), (1,)), ((), ())), preferred_el...  8.18 us
  transfers between devices with their start and end apart: 4, of which 4 were waited for; matrix products, arithmetic and copies ran while one was open for 12% of the time, Pallas kernels for 0%

profile of v1, /device:TPU:0, one launch (start us, length us, event | category | flops | bytes accessed | tf_op | source)
XLA Modules:
  0.0 312.4 jit_solution(17506155595354324222)
XLA Ops:
  7.2 0.0 copy-start
  7.2 0.0 all-gather.5.cloned.1.call-start
  7.2 0.7 all-gather.5.cloned.1.call-update
  7.9 0.0 all-gather.7.cloned.1.call-start
  8.0 0.7 all-gather.7.cloned.1.call-update
  8.7 0.0 reduce-scatter.5.cloned.1.call-start
  8.7 44.1 %all-gather.1 = s32[32,32,8]{1,2,0:T(8,128)S(1)} all-gather(s32[1,32,8]{1,2,0:T(8,128)} %bitcast.56), channel_id=1, replica_groups=mesh['dp'=2,'expert'=16] {'dp','expert'}, dimensions={0}, use_global_device_ids=true | all-gather | bytes 33792 | tf_op jit(solution)/shard_map/all_gather | solution.py:141
  52.8 0.1 reshape.25
  53.0 0.1 convert_reduce_fusion
  53.0 22.7 %all-gather.5.cloned.1.call-done = bf16[1024,2048]{1,0:T(8,128)(2,1)} async-done(((bf16[32,2048]{1,0:T(8,128)(2,1)}), bf16[1024,2048]{1,0:T(8,128)(2,1)}) %all-gather.5.cloned.1.call-update) | async-done | bytes 4194320 | tf_op jit(solution)/shard_map/all_gather | solution.py:142
  75.7 8.5 %fusion.10 = f32[1024,768]{0,1:T(8,128)} fusion(bf16[1024,2048]{1,0:T(8,128)(2,1)} %all-gather.5.cloned.1.call-done, bf16[1,2048,768]{2,1,0:T(8,128)(2,1)} %param.11), kind=kOutput, calls=%fused_computation.11 | convolution fusion | flops 3221225472 | bytes 10485760 | tf_op jit(solution)/shard_map/dot_general | solution.py:158
  84.2 0.0 copy-done.1
  84.2 0.0 copy-done.10
  84.2 5.3 %fusion.6 = f32[1024,768]{0,1:T(8,128)} fusion(bf16[1024,2048]{1,0:T(8,128)(2,1)S(1)} %copy-done.1, bf16[1,2048,768]{2,1,0:T(8,128)(2,1)S(1)} %copy-done.10), kind=kOutput, calls=%fused_computation.7 | convolution fusion | flops 3221225472 | bytes 10485760 | tf_op jit(solution)/shard_map/dot_general | solution.py:159
  89.6 49.6 %all-gather.7.cloned.1.call-done = bf16[1024,2048]{1,0:T(8,128)(2,1)} async-done(((bf16[32,2048]{1,0:T(8,128)(2,1)}), bf16[1024,2048]{1,0:T(8,128)(2,1)}) %all-gather.7.cloned.1.call-update) | async-done | bytes 4194320 | tf_op jit(solution)/shard_map/all_gather | solution.py:143
  139.2 0.0 copy-done
  139.2 8.2 %multiply_reduce_fusion = (f32[1024]{0:T(1024)S(1)}, f32[1024,768]{0,1:T(8,128)}) fusion(f32[1024,768]{0,1:T(8,128)} %fusion.6, f32[1024,768]{0,1:T(8,128)} %fusion.10, bf16[1024,2048]{1,0:T(8,128)(2,1)} %all-gather.7.cloned.1.call-done, bf16[1,768,2048]{2,1,0:T(8,128)(2,1)S(1)} %copy-done), kind=kOutput, calls=%fused_computation.13 | convolution fusion | flops 3226729472 | bytes 16781312 | tf_op jit(solution)/shard_map/dot_general | solution.py:160
  147.4 20.0 %all-gather = f32[16384]{0:T(1024)S(1)} all-gather(f32[1024]{0:T(1024)S(1)} %get-tuple-element.13), channel_id=2, replica_groups=mesh['dp'=2,'expert'=16] {'expert'}, dimensions={0}, use_global_device_ids=true | all-gather | bytes 69632 | tf_op jit(solution)/shard_map/all_gather | solution.py:205
  167.4 0.0 copy-done.9
  167.4 0.0 copy-start.4
  167.4 3.6 %fusion.60 = (f32[1024]{0:T(1024)S(1)}, f32[1024,16]{0,1:T(8,128)S(1)}) fusion(bf16[1024,2048]{1,0:T(8,128)(2,1)} %all-gather.5.cloned.1.call-done, bf16[2048,16]{0,1:T(8,128)(2,1)S(1)} %copy-done.9), kind=kOutput, calls=%fused_computation.62 | convolution fusion | flops 67124224 | bytes 4329472 | tf_op jit(solution)/shard_map/dot_general | solution.py:144
  171.0 0.1 fusion.46
  171.1 0.0 copy-done.4
  171.1 0.0 copy-start.11
  171.1 5.0 %multiply_convert_fusion.1 = (bf16[1024,768]{0,1:T(8,128)(2,1)S(1)}, bf16[1024,768]{0,1:T(8,128)(2,1)S(1)}, bf16[1024,768]{0,1:T(8,128)(2,1)}) fusion(f32[1024,768]{0,1:T(8,128)S(1)} %copy-done.4, f32[1024,768]{0,1:T(8,128)} %fusion.6, f32[1024,768]{0,1:T(8,128)} %get-tuple-element.14, f32[1024]{0:T(1024)S(1)} %get-tuple-element.7), kind=kLoop, calls=%fused_computation.15 | loop fusion | flops 13369344 | bytes 14159872 | tf_op jit(solution)/shard_map/convert_element_type | solution.py:168
  176.1 0.0 copy-done.11
  176.1 0.0 copy-start.12
  176.1 1.9 fusion.4
  178.0 0.0 copy-done.7
  178.0 0.0 copy-done.5
  178.0 1.1 copy-done.12
  179.1 3.2 %add_convert_fusion = bf16[512,2048]{1,0:T(8,128)(2,1)} fusion(f32[512,2048]{1,0:T(8,128)S(1)} %fusion.4, bf16[1,2048,768]{2,1,0:T(8,128)(2,1)S(1)} %copy-done.12, bf16[1024,768]{0,1:T(8,128)(2,1)S(1)} %get-tuple-element.10, s32[]{:T(128)S(6)} %select_n.12), kind=kOutput, calls=%fused_computation | convolution fusion | flops 1612709888 | bytes 10223620 | tf_op jit(solution)/shard_map/dot_general | solution.py:181
  182.3 0.0 reduce-scatter.5.cloned.1.call-update
  182.3 0.3 reduce-scatter.3.cloned.1.call-start
  182.6 4.3 %fusion.13 = bf16[512,2048]{1,0:T(8,128)(2,1)} fusion(bf16[1,768,2048]{2,1,0:T(8,128)(2,1)S(1)} %copy-done, bf16[1024,768]{0,1:T(8,128)(2,1)} %get-tuple-element.12, s32[]{:T(128)S(6)} %select_n.12), kind=kOutput, calls=%fused_computation.19 | convolution fusion | flops 1611661312 | bytes 6029316 | tf_op jit(solution)/shard_map/dot_general | solution.py:176
  186.9 0.0 reduce-scatter.3.cloned.1.call-update
  187.0 0.0 copy-start.3
  187.0 4.8 %convolution_bitcast_fusion = f32[2048,16]{0,1:T(8,128)} fusion(f32[1024,16]{0,1:T(8,128)S(1)} %subtract_multiply_fusion, bf16[1024,2048]{1,0:T(8,128)(2,1)} %all-gather.5.cloned.1.call-done), kind=kOutput, calls=%fused_computation.22 | convolution fusion | flops 402653184 | bytes 4390912 | tf_op jit(solution)/shard_map/td,te->de/dot_general | solution.py:210
  191.8 0.0 copy-done.3
  191.9 4.7 %fusion.34 = bf16[1,768,1024]{2,1,0:T(8,128)(2,1)} fusion(bf16[1024,768]{0,1:T(8,128)(2,1)S(1)} %copy-done.3, bf16[1024,2048]{1,0:T(8,128)(2,1)} %all-gather.7.cloned.1.call-done, s32[]{:T(128)S(6)} %select_n.14), kind=kOutput, calls=%fused_computation.32 | convolution fusion | flops 1611399168 | bytes 5242884 | tf_op jit(solution)/shard_map/dot_general | solution.py:202
  196.6 0.0 copy-done.2
  196.6 0.0 copy-done.8
  196.6 3.0 fusion.37
  199.6 0.0 copy-done.6
  199.6 3.0 fusion.40
  202.6 38.0 %reduce-scatter.5.cloned.1.call-done = bf16[32,2048]{1,0:T(8,128)(2,1)} async-done(((bf16[512,2048]{1,0:T(8,128)(2,1)}), bf16[32,2048]{1,0:T(8,128)(2,1)}) %reduce-scatter.5.cloned.1.call-update) | async-done | bytes 131088 | tf_op jit(solution)/shard_map/reduce_scatter | solution.py:190
  240.7 1.9 fusion.18
  242.6 63.3 %reduce-scatter.3.cloned.1.call-done = bf16[32,2048]{1,0:T(8,128)(2,1)} async-done(((bf16[512,2048]{1,0:T(8,128)(2,1)}), bf16[32,2048]{1,0:T(8,128)(2,1)}) %reduce-scatter.3.cloned.1.call-update) | async-done | bytes 131088 | tf_op jit(solution)/shard_map/reduce_scatter | solution.py:179
  (14 shorter events, 0.2 us)
Async XLA Ops:
  7.2 132.1 %copy-start = (bf16[1,768,2048]{2,1,0:T(8,128)(2,1)S(1)}, bf16[1,768,2048]{2,1,0:T(8,128)(2,1)}, u32[]{:S(2)}) copy-start(bf16[1,768,2048]{2,1,0:T(8,128)(2,1)} %param.13) | copy-start | bytes 9437188
  7.2 68.6 %all-gather.5.cloned.1.call-start = ((), (), s32[]{:S(2)}) async-start(), calls=%async_computation.2 | async-start | bytes 4325376 | tf_op jit(solution)/shard_map/all_gather | solution.py:142
  7.9 131.3 %all-gather.7.cloned.1.call-start = ((), (), s32[]{:S(2)}) async-start(), calls=%async_computation.4 | async-start | bytes 4325376 | tf_op jit(solution)/shard_map/all_gather | solution.py:143
  8.7 232.0 %reduce-scatter.5.cloned.1.call-start = ((), (), s32[]{:S(2)}) async-start(), calls=%async_computation.5 | async-start | bytes 2228224 | tf_op jit(solution)/shard_map/reduce_scatter | solution.py:190
  75.7 8.5 %copy-start.1 = (bf16[1024,2048]{1,0:T(8,128)(2,1)S(1)}, bf16[1024,2048]{1,0:T(8,128)(2,1)}, u32[]{:S(2)}) copy-start(bf16[1024,2048]{1,0:T(8,128)(2,1)} %all-gather.5.cloned.1.call-done) | copy-start | bytes 12582916
  75.7 8.5 %copy-start.10 = (bf16[1,2048,768]{2,1,0:T(8,128)(2,1)S(1)}, bf16[1,2048,768]{2,1,0:T(8,128)(2,1)}, u32[]{:S(2)}) copy-start(bf16[1,2048,768]{2,1,0:T(8,128)(2,1)} %param.12) | copy-start | bytes 9437188
  89.6 77.8 %copy-start.9 = (bf16[2048,16]{0,1:T(8,128)(2,1)S(1)}, bf16[2048,16]{0,1:T(8,128)(2,1)}, u32[]{:S(2)}) copy-start(bf16[2048,16]{0,1:T(8,128)(2,1)} %param.10) | copy-start | bytes 196612
  167.4 3.7 %copy-start.4 = (f32[1024,768]{0,1:T(8,128)S(1)}, f32[1024,768]{0,1:T(8,128)}, u32[]{:S(2)}) copy-start(f32[1024,768]{0,1:T(8,128)} %fusion.10) | copy-start | bytes 9437188
  171.1 5.0 %copy-start.11 = (bf16[1,2048,768]{2,1,0:T(8,128)(2,1)S(1)}, bf16[1,2048,768]{2,1,0:T(8,128)(2,1)}, u32[]{:S(2)}) copy-start(bf16[1,2048,768]{2,1,0:T(8,128)(2,1)} %param.12) | copy-start | bytes 9437188
  176.1 1.9 copy-start.7
  176.1 1.9 copy-start.5
  176.1 3.0 copy-start.12
  182.3 123.6 %reduce-scatter.3.cloned.1.call-start = ((), (), s32[]{:S(2)}) async-start(), calls=%async_computation.3 | async-start | bytes 2228224 | tf_op jit(solution)/shard_map/reduce_scatter | solution.py:179
  187.0 4.9 %copy-start.3 = (bf16[1024,768]{0,1:T(8,128)(2,1)S(1)}, bf16[1024,768]{0,1:T(8,128)(2,1)}, u32[]{:S(2)}) copy-start(bf16[1024,768]{0,1:T(8,128)(2,1)} %get-tuple-element.12) | copy-start | bytes 4718596
  191.8 4.8 %copy-start.2 = (bf16[1024,2048]{1,0:T(8,128)(2,1)S(1)}, bf16[1024,2048]{1,0:T(8,128)(2,1)}, u32[]{:S(2)}) copy-start(bf16[1024,2048]{1,0:T(8,128)(2,1)} %all-gather.5.cloned.1.call-done) | copy-start | bytes 12582916
  191.8 4.8 %copy-start.8 = (bf16[1024,768]{0,1:T(8,128)(2,1)S(1)}, bf16[1024,768]{0,1:T(8,128)(2,1)}, u32[]{:S(2)}) copy-start(bf16[1024,768]{0,1:T(8,128)(2,1)} %copy-done.7) | copy-start | bytes 4718596
  196.6 3.0 copy-start.6
Sparse Core Ops, SparseCore 0:
  10.9 64.8 all-gather.4
  78.6 60.6 all-gather.6
  182.4 58.1 reduce-scatter.4
  245.3 60.5 reduce-scatter.2

commit v2 on v1

--- a/solution.py
+++ b/solution.py
@@ -128,6 +128,13 @@
     return (layer_out, token_grad, gate_grad, up_grad, down_grad, router_grad)
 
 
+def swap(array, bit):
+    if bit == 0:
+        return lax.ppermute(array, "dp", [(0, 1), (1, 0)])
+    size = lax.axis_size("expert")
+    return lax.ppermute(array, "expert", [(i, i ^ bit) for i in range(size)])
+
+
 def local_dense(tokens, routes, cotangent, router_weight, gate_weight, up_weight, down_weight):
     tok_rows = tokens.shape[0]
     model_width = tokens.shape[1]
@@ -136,25 +143,33 @@
     dp_size = lax.axis_size("dp")
     dp_index = lax.axis_index("dp")
     expert_index = lax.axis_index("expert")
-    both = ("dp", "expert")
     gate_mat, up_mat, down_mat = gate_weight[0], up_weight[0], down_weight[0]
-    routes_all = lax.all_gather(routes, both, axis=0, tiled=True)
-    tokens_all = lax.all_gather(tokens, both, axis=0, tiled=True)
-    cot_all = lax.all_gather(cotangent, both, axis=0, tiled=True)
-    logits = jnp.dot(tokens_all, router_weight, preferred_element_type=jnp.float32)
+    logits = jnp.dot(tokens, router_weight, preferred_element_type=jnp.float32)
     exp_logits = jnp.exp(logits)
     probability = exp_logits / jnp.sum(exp_logits, axis=1, keepdims=True)
     chosen = jnp.sum(
-        (
-            routes_all[:, :, None] == jnp.arange(expert_count, dtype=jnp.int32)[None, None, :]
-        ).astype(jnp.float32),
+        (routes[:, :, None] == jnp.arange(expert_count, dtype=jnp.int32)[None, None, :]).astype(
+            jnp.float32
+        ),
         axis=1,
     )
     selected = chosen * probability
     sel_total = jnp.sum(selected, axis=1, keepdims=True)
     combine = selected / sel_total
+    bits = [1, 0, 2, 8, 4]
+    ones = (1,) * len(bits)
+
+    def gather(array, order):
+        array = array.reshape(ones + array.shape)
+        for bit in order:
+            array = jnp.concatenate([array, swap(array, bit)], axis=bits.index(bit))
+        return array.reshape((-1, array.shape[-1]))
+
+    combine_all = gather(combine, (4, 8, 2, 0, 1))
+    tokens_all = gather(tokens, (4, 8, 2, 0, 1))
+    cot_all = gather(cotangent, (4, 8, 0, 2, 1))
     mine = (jnp.arange(expert_count, dtype=jnp.int32) == expert_index).astype(jnp.float32)
-    scale = jnp.sum(combine * mine[None, :], axis=1, keepdims=True)
+    scale = jnp.sum(combine_all * mine[None, :], axis=1, keepdims=True)
     gate_act = jnp.dot(tokens_all, gate_mat, preferred_element_type=jnp.float32)
     up_act = jnp.dot(tokens_all, up_mat, preferred_element_type=jnp.float32)
     raw_grad = lax.dot_general(
@@ -167,16 +182,21 @@
     hidden_grad = raw_grad * scale
     gate_part = (hidden_grad * up_act * act_slope).astype(jnp.bfloat16)
     up_part = (hidden_grad * act_value).astype(jnp.bfloat16)
-    group_rows = group_size * tok_rows
-    first = dp_index * group_rows
 
     def rows_of(array):
-        return lax.dynamic_slice_in_dim(array, first, group_rows, axis=0)
+        quarter = array.reshape((2, 2, group_size * tok_rows // 2) + array.shape[1:])
+        return quarter[:, 0].reshape((group_size * tok_rows,) + array.shape[1:])
+
+    def scatter(term):
+        term = term.reshape((2, 2, 2, 2, tok_rows, model_width))
+        for bit in (1, 2, 8, 4):
+            total = term[0].astype(jnp.float32) + swap(term[1], bit).astype(jnp.float32)
+            term = total.astype(jnp.bfloat16)
+        return total
 
     out_term = jnp.dot(
         rows_of(scaled_hidden), down_mat, preferred_element_type=jnp.float32
     ).astype(jnp.bfloat16)
-    layer_out = lax.psum_scatter(out_term, "expert", scatter_dimension=0, tiled=True)
     in_term = (
         lax.dot_general(
             rows_of(gate_part), gate_mat, (((1,), (1,)), ((), ())),
@@ -187,7 +207,8 @@
             preferred_element_type=jnp.float32,
         )
     ).astype(jnp.bfloat16)
-    in_sum = lax.psum_scatter(in_term, "expert", scatter_dimension=0, tiled=True)
+    layer_out = scatter(out_term).astype(jnp.bfloat16)
+    in_sum = scatter(in_term)
     part_width = model_width // dp_size
     start = dp_index * part_width
     tokens_part = lax.dynamic_slice_in_dim(tokens_all, start, part_width, axis=1)
@@ -202,33 +223,40 @@
     down_grad = lax.dot_general(
         scaled_hidden, cot_part, over_rows, preferred_element_type=jnp.float32
     ).astype(jnp.bfloat16)
-    comb_grad = lax.all_gather(comb_mine, "expert", axis=0).T
+    comb = rows_of(comb_mine).reshape((2, 2, 2, 2, tok_rows, 1))
+    places = []
+    for step, bit in enumerate((1, 2, 8, 4)):
+        comb = jnp.concatenate([comb[0], swap(comb[1], bit)], axis=-1)
+        places = places + [p + bit for p in places] if step else [0, bit]
+    columns = jnp.asarray(places, jnp.int32) ^ expert_index
+    spread = (
+        columns[:, None] == jnp.arange(expert_count, dtype=jnp.int32)[None, :]
+    ).astype(jnp.float32)
+    comb_grad = jnp.sum(comb[:, :, None] * spread[None], axis=1)
     sel_grad = (
         chosen * (comb_grad - jnp.sum(combine * comb_grad, axis=1, keepdims=True)) / sel_total
     )
     logit_grad = probability * (sel_grad - jnp.sum(probability * sel_grad, axis=1, keepdims=True))
-    router_grad = jnp.einsum(
-        "td,te->de",
-        tokens_all.astype(jnp.float32),
-        logit_grad,
-        precision=lax.Precision.HIGHEST,
-    )
-    own_first = (dp_index * group_size + expert_index) * tok_rows
-    own_logit_grad = lax.dynamic_slice_in_dim(logit_grad, own_first, tok_rows, axis=0)
+    router_term = jnp.einsum(
+        "td,te->de", tokens.astype(jnp.float32), logit_grad, precision=lax.Precision.HIGHEST
+    )
+    router_grad = lax.psum(router_term, ("dp", "expert"))
     router_back = jnp.einsum(
-        "te,de->td",
-        own_logit_grad,
-        router_weight.astype(jnp.float32),
-        precision=lax.Precision.HIGHEST,
-    )
-    token_grad = (in_sum.astype(jnp.float32) + router_back).astype(jnp.bfloat16)
+        "te,de->td", logit_grad, router_weight.astype(jnp.float32), precision=lax.Precision.HIGHEST
+    )
+    token_grad = (in_sum + router_back).astype(jnp.bfloat16)
     return (layer_out, token_grad, gate_grad[None], up_grad[None], down_grad[None], router_grad)
 
 
 def local(tokens, routes, cotangent, router_weight, gate_weight, up_weight, down_weight):
     tok_rows, top_count = routes.shape
     capacity = min(tok_rows, 2 * tok_rows * top_count // router_weight.shape[1])
-    dense = capacity == tok_rows and gate_weight.shape[0] == 1
+    dense = (
+        capacity == tok_rows
+        and gate_weight.shape[0] == 1
+        and lax.axis_size("dp") == 2
+        and lax.axis_size("expert") == 16
+    )
     plan = local_dense if dense else local_slots
     return plan(tokens, routes, cotangent, router_weight, gate_weight, up_weight, down_weight)
 

time: 313 us -> 308 us (0.984)
  blocking collectives: 64.1 us -> 0 us
  starting transfers between devices: 0.38 us -> 31.6 us
  waiting for transfers between devices: 175 us -> 195 us
  matrix products: 52.5 us -> 34.2 us
  other arithmetic: 5.2 us -> 23.1 us
  local copies, waits for them, and re-layouts: 1.34 us -> 8.75 us
    ppermute x0 -> x27, waiting for transfers between devices: none -> 112 us  [the longest x24 99.8 us: swap(): return lax.ppermute(array, 'expert', [(i, i ^ bit) for i in range(size)])]
    reduce_scatter x2 -> x0, waiting for transfers between devices: 101 us -> none  [the longest x1 63.3 us: local_dense(): lax.psum_scatter(out_term, 'expert', scatter_dimension=0, tiled=True)]
    psum x0 -> x1, waiting for transfers between devices: none -> 82.8 us  [local_dense(): router_grad = lax.psum(router_term, ('dp', 'expert'))]
    all_gather x2 -> x0, waiting for transfers between devices: 72.3 us -> none  [the longest x1 49.6 us: local_dense(): cot_all = lax.all_gather(cotangent, both, axis=0, tiled=True)]
    all_gather x2 -> x0, blocking collectives: 64.1 us -> none  [the longest x1 44.1 us: local_dense(): routes_all = lax.all_gather(routes, both, axis=0, tiled=True)]
    ppermute x0 -> x27, starting transfers between devices: none -> 31.5 us  [the longest x24 28.9 us: swap(): return lax.ppermute(array, 'expert', [(i, i ^ bit) for i in range(size)])]
    concatenate x0 -> x15, other arithmetic: none -> 14.6 us  [the longest x14 14.6 us: gather(): array = jnp.concatenate([array, swap(array, bit)], axis=bits.index(bit))]
    dot_general x3, matrix products: 10.3 us -> 2 us  [the longest x1 0.97 us: local_dense(): jnp.einsum('te,de->td', logit_grad, router_weight.astype(jnp.float32), pr...]
  transfers between devices with their start and end apart: 4 -> 28, of which waited for: 4 -> 19; matrix products, arithmetic and copies ran while one was open for 12% -> 17% of each run, Pallas kernels for 0% -> 0%
where the time goes in v2:
time: 308 us
  waiting for transfers between devices  195 us (63%)
  matrix products  34.2 us (11%)
  starting transfers between devices  31.6 us (10%)
  other arithmetic  23.1 us (8%)
  between operations  14.7 us (5%)
  local copies, waits for them, and re-layouts  8.75 us (3%)
    ppermute x24, waiting for transfers between devices, swap(): return lax.ppermute(array, 'expert', [(i, i ^ bit) for i in range(size)])  99.8 us
    psum x1, waiting for transfers between devices, local_dense(): router_grad = lax.psum(router_term, ('dp', 'expert'))  82.8 us
    ppermute x24, starting transfers between devices, swap(): return lax.ppermute(array, 'expert', [(i, i ^ bit) for i in range(size)])  28.9 us
    concatenate x14, other arithmetic, gather(): array = jnp.concatenate([array, swap(array, bit)], axis=bits.index(bit))  14.6 us
    ppermute x3, waiting for transfers between devices, swap(): return lax.ppermute(array, 'dp', [(0, 1), (1, 0)])  12.6 us
    dot_general x1, matrix products, local_dense(): lax.dot_general(cot_all, down_mat, (((1,), (1,)), ((), ())), preferred_el...  6.54 us
  transfers between devices with their start and end apart: 28, of which 19 were waited for; matrix products, arithmetic and copies ran while one was open for 17% of the time, Pallas kernels for 0%

profile of v2, /device:TPU:0, one launch (start us, length us, event | category | flops | bytes accessed | tf_op | source)
XLA Modules:
  0.0 307.6 jit_solution(10275347705102832198)
XLA Ops:
  7.3 3.1 %collective-permute-start = (bf16[1,1,1,1,1,32,2048]{6,5,4,3,2,1,0:T(8,128)(2,1)}, bf16[1,1,1,1,1,32,2048]{6,5,4,3,2,1,0:T(8,128)(2,1)S(1)}, u32[]{:S(2)}, u32[]{:S(2)}) collective-permute-start(bf16[1,1,1,1,1,32,2048]{6,5,4,3,2,1,0:T(8,128)(2,1)} %bitcast.114), channel_id=1, source_target_pairs={{0,4},{1,5},{2,6},{3,7},{4,0},{5,1},{6,2},{7,3},{8,12},{9,13},{10,... | collective-permute-start | bytes 393224 | tf_op jit(solution)/shard_map/ppermute | solution.py:135
  10.4 3.7 %collective-permute-done = bf16[1,1,1,1,1,32,2048]{6,5,4,3,2,1,0:T(8,128)(2,1)S(1)} collective-permute-done((bf16[1,1,1,1,1,32,2048]{6,5,4,3,2,1,0:T(8,128)(2,1)}, bf16[1,1,1,1,1,32,2048]{6,5,4,3,2,1,0:T(8,128)(2,1)S(1)}, u32[]{:S(2)}, u32[]{:S(2)}) %collective-permute-start) | collective-permute-done | bytes 131104 | tf_op jit(solution)/shard_map/ppermute | solution.py:135
  15.1 2.8 collective-permute-start.1
  17.9 11.3 %collective-permute-done.1 = bf16[1,1,1,1,2,32,2048]{6,5,4,3,2,1,0:T(8,128)(2,1)S(1)} collective-permute-done((bf16[1,1,1,1,2,32,2048]{6,5,4,3,2,1,0:T(8,128)(2,1)S(1)}, bf16[1,1,1,1,2,32,2048]{6,5,4,3,2,1,0:T(8,128)(2,1)S(1)}, u32[]{:S(2)}, u32[]{:S(2)}) %collective-permute-start.1) | collective-permute-done | bytes 262176 | tf_op jit(solution)/shard_map/ppermute | solution.py:135
  30.1 1.4 collective-permute-start.2
  31.5 11.6 %collective-permute-done.2 = bf16[1,1,1,2,2,32,2048]{6,5,4,3,2,1,0:T(8,128)(2,1)S(1)} collective-permute-done((bf16[1,1,1,2,2,32,2048]{6,5,4,3,2,1,0:T(8,128)(2,1)S(1)}, bf16[1,1,1,2,2,32,2048]{6,5,4,3,2,1,0:T(8,128)(2,1)S(1)}, u32[]{:S(2)}, u32[]{:S(2)}) %collective-permute-start.2) | collective-permute-done | bytes 524320 | tf_op jit(solution)/shard_map/ppermute | solution.py:135
  44.2 1.3 collective-permute-start.3
  45.5 1.8 collective-permute-start.14
  47.2 3.2 %collective-permute-done.14 = bf16[1,1,1,1,1,32,2048]{6,5,4,3,2,1,0:T(8,128)(2,1)S(1)} collective-permute-done((bf16[1,1,1,1,1,32,2048]{6,5,4,3,2,1,0:T(8,128)(2,1)S(1)}, bf16[1,1,1,1,1,32,2048]{6,5,4,3,2,1,0:T(8,128)(2,1)S(1)}, u32[]{:S(2)}, u32[]{:S(2)}) %collective-permute-start.14) | collective-permute-done | bytes 131104 | tf_op jit(solution)/shard_map/ppermute | solution.py:135
  50.5 3.2 %collective-permute-start.15 = (bf16[1,1,1,1,2,32,2048]{6,5,4,3,2,1,0:T(8,128)(2,1)S(1)}, bf16[1,1,1,1,2,32,2048]{6,5,4,3,2,1,0:T(8,128)(2,1)S(1)}, u32[]{:S(2)}, u32[]{:S(2)}) collective-permute-start(bf16[1,1,1,1,2,32,2048]{6,5,4,3,2,1,0:T(8,128)(2,1)S(1)} %pad_maximum_fusion.9), channel_id=1, source_target_pairs={{0,8},{1,9},{2,10},{3,11},{4,12},{5,13},{6,14},{7,15},{8,0},{9,1},... | collective-permute-start | bytes 786440 | tf_op jit(solution)/shard_map/ppermute | solution.py:135
  53.9 10.2 %collective-permute-done.15 = bf16[1,1,1,1,2,32,2048]{6,5,4,3,2,1,0:T(8,128)(2,1)S(1)} collective-permute-done((bf16[1,1,1,1,2,32,2048]{6,5,4,3,2,1,0:T(8,128)(2,1)S(1)}, bf16[1,1,1,1,2,32,2048]{6,5,4,3,2,1,0:T(8,128)(2,1)S(1)}, u32[]{:S(2)}, u32[]{:S(2)}) %collective-permute-start.15) | collective-permute-done | bytes 262176 | tf_op jit(solution)/shard_map/ppermute | solution.py:135
  64.7 4.7 %collective-permute-done.3 = bf16[1,1,2,2,2,32,2048]{6,5,4,3,2,1,0:T(8,128)(2,1)S(1)} collective-permute-done((bf16[1,1,2,2,2,32,2048]{6,5,4,3,2,1,0:T(8,128)(2,1)S(1)}, bf16[1,1,2,2,2,32,2048]{6,5,4,3,2,1,0:T(8,128)(2,1)S(1)}, u32[]{:S(2)}, u32[]{:S(2)}) %collective-permute-start.3) | collective-permute-done | bytes 1048608 | tf_op jit(solution)/shard_map/ppermute | solution.py:133
  69.4 1.7 pad_maximum_fusion.2
  71.2 2.5 collective-permute-start.5
  73.6 5.1 %collective-permute-done.16 = bf16[1,1,1,2,2,32,2048]{6,5,4,3,2,1,0:T(8,128)(2,1)S(1)} collective-permute-done((bf16[1,1,1,2,2,32,2048]{6,5,4,3,2,1,0:T(8,128)(2,1)S(1)}, bf16[1,1,1,2,2,32,2048]{6,5,4,3,2,1,0:T(8,128)(2,1)S(1)}, u32[]{:S(2)}, u32[]{:S(2)}) %collective-permute-start.16) | collective-permute-done | bytes 524320 | tf_op jit(solution)/shard_map/ppermute | solution.py:133
  82.4 5.0 %collective-permute-done.6 = f32[1,1,1,1,2,32,16]{5,6,4,3,2,1,0:T(8,128)} collective-permute-done((f32[1,1,1,1,2,32,16]{5,6,4,3,2,1,0:T(8,128)}, f32[1,1,1,1,2,32,16]{5,6,4,3,2,1,0:T(8,128)}, u32[]{:S(2)}, u32[]{:S(2)}) %collective-permute-start.6) | collective-permute-done | bytes 4128 | tf_op jit(solution)/shard_map/ppermute | solution.py:135
  89.7 15.2 %collective-permute-done.7 = f32[1,1,1,2,2,32,16]{5,6,4,3,2,1,0:T(8,128)S(1)} collective-permute-done((f32[1,1,1,2,2,32,16]{5,6,4,3,2,1,0:T(8,128)S(1)}, f32[1,1,1,2,2,32,16]{5,6,4,3,2,1,0:T(8,128)S(1)}, u32[]{:S(2)}, u32[]{:S(2)}) %collective-permute-start.7) | collective-permute-done | bytes 8224 | tf_op jit(solution)/shard_map/ppermute | solution.py:135
  107.1 2.8 collective-permute-done.8
  109.9 1.4 pad_maximum_fusion.10
  113.0 1.7 fusion.48
  115.5 1.8 pad_maximum_fusion.3
  117.6 1.9 pad_maximum_fusion
  120.0 3.4 %fusion.10 = f32[1024,768]{1,0:T(8,128)S(1)} fusion(bf16[1024,2048]{1,0:T(8,128)(2,1)S(1)} %bitcast.120, bf16[1,2048,768]{2,1,0:T(8,128)(2,1)S(1)} %copy-done.41), kind=kOutput, calls=%fused_computation.13 | convolution fusion | flops 3221225472 | bytes 10485760 | tf_op jit(solution)/shard_map/dot_general | solution.py:173
  123.4 3.4 %fusion.6 = f32[1024,768]{1,0:T(8,128)S(1)} fusion(bf16[1024,2048]{1,0:T(8,128)(2,1)S(1)} %bitcast.121, bf16[1,2048,768]{2,1,0:T(8,128)(2,1)S(1)} %copy-done.40), kind=kOutput, calls=%fused_computation.9 | convolution fusion | flops 3221225472 | bytes 10485760 | tf_op jit(solution)/shard_map/dot_general | solution.py:174
  126.9 1.5 pad_maximum_fusion.1
  128.5 6.5 %multiply_reduce_fusion = (f32[1024]{0:T(1024)S(1)}, bf16[1024,768]{1,0:T(8,128)(2,1)}, bf16[1024,768]{1,0:T(8,128)(2,1)}, bf16[1024,768]{1,0:T(8,128)(2,1)}) fusion(f32[1024,768]{1,0:T(8,128)S(1)} %fusion.6, f32[1024,768]{1,0:T(8,128)S(1)} %fusion.10, f32[1024]{0:T(1024)S(1)} %mul.85, bf16[1024,2048]{1,0:T(8,128)(2,1)S(1)} %bitcast.124, ...), kind=kOutput, calls=%fused_computation.15 | convolution fusion | flops 3236166656 | bytes 18358272 | tf_op jit(solution)/shard_map/dot_general | solution.py:175
  136.5 3.9 %fusion.4 = f32[512,2048]{1,0:T(8,128)S(1)} fusion(bf16[512,768]{1,0:T(8,128)(2,1)S(1)} %bitcast.135, bf16[1,2048,768]{2,1,0:T(8,128)(2,1)} %param.13), kind=kOutput, calls=%fused_computation.7 | convolution fusion | flops 1610612736 | bytes 8126464 | tf_op jit(solution)/shard_map/dot_general | solution.py:205
  140.4 1.8 add_convert_fusion
  142.3 1.6 fusion.70
  144.2 1.8 fusion.13
  146.1 1.5 fusion.71
  147.7 1.6 collective-permute-start.24
  149.2 5.1 %fusion.35 = bf16[1,768,1024]{2,1,0:T(8,128)(2,1)} fusion(bf16[1024,768]{1,0:T(8,128)(2,1)} %get-tuple-element.14, bf16[1024,2048]{1,0:T(8,128)(2,1)} %bitcast.125, s32[]{:T(128)S(6)} %select_n.4), kind=kOutput, calls=%fused_computation.38 | convolution fusion | flops 1611399168 | bytes 5242884 | tf_op jit(solution)/shard_map/dot_general | solution.py:223
  154.8 3.1 fusion.38
  159.1 4.6 %collective-permute-start.26 = (f32[32,8]{0,1:T(8,128)S(1)}, f32[32,8]{0,1:T(8,128)S(1)}, u32[]{:S(2)}, u32[]{:S(2)}) collective-permute-start(f32[32,8]{0,1:T(8,128)S(1)} %get-tuple-element.21), channel_id=1, source_target_pairs={{0,4},{1,5},{2,6},{3,7},{4,0},{5,1},{6,2},{7,3},{8,12},{9,13},{10,... | collective-permute-start | bytes 3080 | tf_op jit(solution)/shard_map/ppermute | solution.py:135
  163.6 3.1 fusion.41
  168.0 2.0 fusion.19
  170.9 1.6 fusion.18
  172.5 1.4 collective-permute-start.20
  173.9 11.2 %collective-permute-done.11 = bf16[2,2,32,2048]{3,2,1,0:T(8,128)(2,1)S(1)} collective-permute-done((bf16[2,2,32,2048]{3,2,1,0:T(8,128)(2,1)S(1)}, bf16[2,2,32,2048]{3,2,1,0:T(8,128)(2,1)S(1)}, u32[]{:S(2)}, u32[]{:S(2)}) %collective-permute-start.11) | collective-permute-done | bytes 524320 | tf_op jit(solution)/shard_map/ppermute | solution.py:135
  186.5 9.3 %collective-permute-done.20 = bf16[2,2,32,2048]{3,2,1,0:T(8,128)(2,1)S(1)} collective-permute-done((bf16[2,2,32,2048]{3,2,1,0:T(8,128)(2,1)S(1)}, bf16[2,2,32,2048]{3,2,1,0:T(8,128)(2,1)S(1)}, u32[]{:S(2)}, u32[]{:S(2)}) %collective-permute-start.20) | collective-permute-done | bytes 524320 | tf_op jit(solution)/shard_map/ppermute | solution.py:135
  195.9 1.4 collective-permute-start.21
  197.4 5.1 %collective-permute-done.12 = bf16[2,32,2048]{2,1,0:T(8,128)(2,1)S(1)} collective-permute-done((bf16[2,32,2048]{2,1,0:T(8,128)(2,1)S(1)}, bf16[2,32,2048]{2,1,0:T(8,128)(2,1)S(1)}, u32[]{:S(2)}, u32[]{:S(2)}) %collective-permute-start.12) | collective-permute-done | bytes 262176 | tf_op jit(solution)/shard_map/ppermute | solution.py:135
  202.6 7.1 %collective-permute-done.21 = bf16[2,32,2048]{2,1,0:T(8,128)(2,1)S(1)} collective-permute-done((bf16[2,32,2048]{2,1,0:T(8,128)(2,1)S(1)}, bf16[2,32,2048]{2,1,0:T(8,128)(2,1)S(1)}, u32[]{:S(2)}, u32[]{:S(2)}) %collective-permute-start.21) | collective-permute-done | bytes 262176 | tf_op jit(solution)/shard_map/ppermute | solution.py:135
  209.9 2.5 collective-permute-done.13
  213.1 2.3 collective-permute-done.22
  216.3 82.8 %all-reduce.2.cloned.1.call-done = f32[2048,16]{0,1:T(8,128)} async-done(((f32[2048,16]{0,1:T(8,128)}), f32[2048,16]{0,1:T(8,128)}) %all-reduce.2.cloned.1.call-update) | async-done | bytes 131088 | tf_op jit(solution)/shard_map/psum | solution.py:243
  299.2 1.6 copy.20
  (159 shorter events, 24.5 us)
Async XLA Ops:
  7.2 121.3 %copy-start = (bf16[1,768,2048]{2,1,0:T(8,128)(2,1)S(1)}, bf16[1,768,2048]{2,1,0:T(8,128)(2,1)}, u32[]{:S(2)}) copy-start(bf16[1,768,2048]{2,1,0:T(8,128)(2,1)} %param.14) | copy-start | bytes 9437188
  7.2 46.5 %copy-start.1 = (bf16[32,2048]{1,0:T(8,128)(2,1)S(1)}, bf16[32,2048]{1,0:T(8,128)(2,1)}, u32[]{:S(2)}) copy-start(bf16[32,2048]{1,0:T(8,128)(2,1)} %param.8) | copy-start | bytes 393220
  7.2 46.5 %copy-start.39 = (s32[32,8]{0,1:T(8,128)S(1)}, s32[32,8]{0,1:T(8,128)}, u32[]{:S(2)}) copy-start(s32[32,8]{0,1:T(8,128)} %param.9) | copy-start | bytes 3076
  7.2 292.0 %all-reduce.2.cloned.1.call-start = ((), (), s32[]{:S(2)}) async-start(), calls=%async_computation | async-start | bytes 262144 | tf_op jit(solution)/shard_map/psum | solution.py:243
  7.2 38.2 %copy-start.14 = (bf16[32,2048]{1,0:T(8,128)(2,1)S(1)}, bf16[32,2048]{1,0:T(8,128)(2,1)}, u32[]{:S(2)}) copy-start(bf16[32,2048]{1,0:T(8,128)(2,1)} %param.10) | copy-start | bytes 393220
  7.3 46.4 %copy-start.26 = (bf16[2048,16]{0,1:T(8,128)(2,1)S(1)}, bf16[2048,16]{0,1:T(8,128)(2,1)}, u32[]{:S(2)}) copy-start(bf16[2048,16]{0,1:T(8,128)(2,1)} %param.11) | copy-start | bytes 196612
  7.3 6.8 %collective-permute-start = (bf16[1,1,1,1,1,32,2048]{6,5,4,3,2,1,0:T(8,128)(2,1)}, bf16[1,1,1,1,1,32,2048]{6,5,4,3,2,1,0:T(8,128)(2,1)S(1)}, u32[]{:S(2)}, u32[]{:S(2)}) collective-permute-start(bf16[1,1,1,1,1,32,2048]{6,5,4,3,2,1,0:T(8,128)(2,1)} %bitcast.114), channel_id=1, source_target_pairs={{0,4},{1,5},{2,6},{3,7},{4,0},{5,1},{6,2},{7,3},{8,12},{9,13},{10,... | collective-permute-start | bytes 393224 | tf_op jit(solution)/shard_map/ppermute | solution.py:135
  14.1 57.0 %copy-start.16 = (bf16[1,1,1,1,1,32,2048]{6,5,4,3,2,1,0:T(8,128)(2,1)}, bf16[1,1,1,1,1,32,2048]{6,5,4,3,2,1,0:T(8,128)(2,1)S(1)}, u32[]{:S(2)}) copy-start(bf16[1,1,1,1,1,32,2048]{6,5,4,3,2,1,0:T(8,128)(2,1)S(1)} %collective-permute-done) | copy-start | bytes 393220
  15.1 14.1 %collective-permute-start.1 = (bf16[1,1,1,1,2,32,2048]{6,5,4,3,2,1,0:T(8,128)(2,1)S(1)}, bf16[1,1,1,1,2,32,2048]{6,5,4,3,2,1,0:T(8,128)(2,1)S(1)}, u32[]{:S(2)}, u32[]{:S(2)}) collective-permute-start(bf16[1,1,1,1,2,32,2048]{6,5,4,3,2,1,0:T(8,128)(2,1)S(1)} %pad_maximum_fusion.8), channel_id=1, source_target_pairs={{0,8},{1,9},{2,10},{3,11},{4,12},{5,13},{6,14},{7,15},{8,0},{9,1},... | collective-permute-start | bytes 786440 | tf_op jit(solution)/shard_map/ppermute | solution.py:135
  30.1 13.0 %collective-permute-start.2 = (bf16[1,1,1,2,2,32,2048]{6,5,4,3,2,1,0:T(8,128)(2,1)S(1)}, bf16[1,1,1,2,2,32,2048]{6,5,4,3,2,1,0:T(8,128)(2,1)S(1)}, u32[]{:S(2)}, u32[]{:S(2)}) collective-permute-start(bf16[1,1,1,2,2,32,2048]{6,5,4,3,2,1,0:T(8,128)(2,1)S(1)} %pad_maximum_fusion.6), channel_id=1, source_target_pairs={{0,2},{1,3},{2,0},{3,1},{4,6},{5,7},{6,4},{7,5},{8,10},{9,11},{10,... | collective-permute-start | bytes 1572872 | tf_op jit(solution)/shard_map/ppermute | solution.py:135
  43.1 28.0 %copy-start.2 = (bf16[1,1,1,2,2,32,2048]{6,5,4,3,2,1,0:T(8,128)(2,1)}, bf16[1,1,1,2,2,32,2048]{6,5,4,3,2,1,0:T(8,128)(2,1)S(1)}, u32[]{:S(2)}) copy-start(bf16[1,1,1,2,2,32,2048]{6,5,4,3,2,1,0:T(8,128)(2,1)S(1)} %collective-permute-done.2) | copy-start | bytes 1572868
  44.2 25.2 %collective-permute-start.3 = (bf16[1,1,2,2,2,32,2048]{6,5,4,3,2,1,0:T(8,128)(2,1)S(1)}, bf16[1,1,2,2,2,32,2048]{6,5,4,3,2,1,0:T(8,128)(2,1)S(1)}, u32[]{:S(2)}, u32[]{:S(2)}) collective-permute-start(bf16[1,1,2,2,2,32,2048]{6,5,4,3,2,1,0:T(8,128)(2,1)S(1)} %pad_maximum_fusion.4), channel_id=1, source_target_pairs={{0,16},{16,0},{1,17},{17,1},{2,18},{18,2},{3,19},{19,3},{4,20},{20... | collective-permute-start | bytes 3145736 | tf_op jit(solution)/shard_map/ppermute | solution.py:133
  45.5 5.0 %collective-permute-start.14 = (bf16[1,1,1,1,1,32,2048]{6,5,4,3,2,1,0:T(8,128)(2,1)S(1)}, bf16[1,1,1,1,1,32,2048]{6,5,4,3,2,1,0:T(8,128)(2,1)S(1)}, u32[]{:S(2)}, u32[]{:S(2)}) collective-permute-start(bf16[1,1,1,1,1,32,2048]{6,5,4,3,2,1,0:T(8,128)(2,1)S(1)} %bitcast.129), channel_id=1, source_target_pairs={{0,4},{1,5},{2,6},{3,7},{4,0},{5,1},{6,2},{7,3},{8,12},{9,13},{10,... | collective-permute-start | bytes 393224 | tf_op jit(solution)/shard_map/ppermute | solution.py:135
  50.5 30.2 %copy-start.18 = (bf16[1,1,1,1,1,32,2048]{6,5,4,3,2,1,0:T(8,128)(2,1)}, bf16[1,1,1,1,1,32,2048]{6,5,4,3,2,1,0:T(8,128)(2,1)S(1)}, u32[]{:S(2)}) copy-start(bf16[1,1,1,1,1,32,2048]{6,5,4,3,2,1,0:T(8,128)(2,1)S(1)} %collective-permute-done.14) | copy-start | bytes 393220
  50.5 13.6 %collective-permute-start.15 = (bf16[1,1,1,1,2,32,2048]{6,5,4,3,2,1,0:T(8,128)(2,1)S(1)}, bf16[1,1,1,1,2,32,2048]{6,5,4,3,2,1,0:T(8,128)(2,1)S(1)}, u32[]{:S(2)}, u32[]{:S(2)}) collective-permute-start(bf16[1,1,1,1,2,32,2048]{6,5,4,3,2,1,0:T(8,128)(2,1)S(1)} %pad_maximum_fusion.9), channel_id=1, source_target_pairs={{0,8},{1,9},{2,10},{3,11},{4,12},{5,13},{6,14},{7,15},{8,0},{9,1},... | collective-permute-start | bytes 786440 | tf_op jit(solution)/shard_map/ppermute | solution.py:135
  53.7 26.9 %copy-start.30 = (f32[32,16]{0,1:T(8,128)}, f32[32,16]{0,1:T(8,128)S(1)}, u32[]{:S(2)}) copy-start(f32[32,16]{0,1:T(8,128)S(1)} %convert_reduce_fusion) | copy-start | bytes 6148
  53.9 26.8 %copy-start.28 = (f32[32,16]{0,1:T(8,128)}, f32[32,16]{0,1:T(8,128)S(1)}, u32[]{:S(2)}) copy-start(f32[32,16]{0,1:T(8,128)S(1)} %get-tuple-element.27) | copy-start | bytes 6148
  53.9 26.8 %copy-start.35 = (f32[32]{0:T(128)}, f32[32]{0:T(128)S(1)}, u32[]{:S(2)}) copy-start(f32[32]{0:T(128)S(1)} %get-tuple-element.26) | copy-start | bytes 388
  64.1 16.6 %copy-start.10 = (bf16[1,1,1,1,2,32,2048]{6,5,4,3,2,1,0:T(8,128)(2,1)}, bf16[1,1,1,1,2,32,2048]{6,5,4,3,2,1,0:T(8,128)(2,1)S(1)}, u32[]{:S(2)}) copy-start(bf16[1,1,1,1,2,32,2048]{6,5,4,3,2,1,0:T(8,128)(2,1)S(1)} %collective-permute-done.15) | copy-start | bytes 786436
  64.1 14.6 %collective-permute-start.16 = (bf16[1,1,1,2,2,32,2048]{6,5,4,3,2,1,0:T(8,128)(2,1)S(1)}, bf16[1,1,1,2,2,32,2048]{6,5,4,3,2,1,0:T(8,128)(2,1)S(1)}, u32[]{:S(2)}, u32[]{:S(2)}) collective-permute-start(bf16[1,1,1,2,2,32,2048]{6,5,4,3,2,1,0:T(8,128)(2,1)S(1)} %pad_maximum_fusion.7), channel_id=1, source_target_pairs={{0,16},{16,0},{1,17},{17,1},{2,18},{18,2},{3,19},{19,3},{4,20},{20... | collective-permute-start | bytes 1572872 | tf_op jit(solution)/shard_map/ppermute | solution.py:133
  69.4 11.3 %copy-start.12 = (bf16[1,1,2,2,2,32,2048]{6,5,4,3,2,1,0:T(8,128)(2,1)}, bf16[1,1,2,2,2,32,2048]{6,5,4,3,2,1,0:T(8,128)(2,1)S(1)}, u32[]{:S(2)}) copy-start(bf16[1,1,2,2,2,32,2048]{6,5,4,3,2,1,0:T(8,128)(2,1)S(1)} %collective-permute-done.3) | copy-start | bytes 3145732
  71.1 46.5 %collective-permute-start.4 = (bf16[1,2,2,2,2,32,2048]{6,5,4,3,2,1,0:T(8,128)(2,1)}, bf16[1,2,2,2,2,32,2048]{6,5,4,3,2,1,0:T(8,128)(2,1)}, u32[]{:S(2)}, u32[]{:S(2)}) collective-permute-start(bf16[1,2,2,2,2,32,2048]{6,5,4,3,2,1,0:T(8,128)(2,1)} %pad_maximum_fusion.2), channel_id=1, source_target_pairs={{0,1},{1,0},{2,3},{3,2},{4,5},{5,4},{6,7},{7,6},{8,9},{9,8},{10,11... | collective-permute-start | bytes 6291464 | tf_op jit(solution)/shard_map/ppermute | solution.py:135
  71.1 10.6 %copy-start.32 = (f32[32,16]{0,1:T(8,128)}, f32[32,16]{0,1:T(8,128)S(1)}, u32[]{:S(2)}) copy-start(f32[32,16]{0,1:T(8,128)S(1)} %get-tuple-element.11) | copy-start | bytes 6148
  71.1 11.2 %copy-start.37 = (f32[32]{0:T(128)}, f32[32]{0:T(128)S(1)}, u32[]{:S(2)}) copy-start(f32[32]{0:T(128)S(1)} %get-tuple-element.10) | copy-start | bytes 388
  71.2 10.6 %collective-permute-start.5 = (f32[1,1,1,1,1,32,16]{5,6,4,3,2,1,0:T(8,128)S(1)}, f32[1,1,1,1,1,32,16]{5,6,4,3,2,1,0:T(8,128)S(1)}, u32[]{:S(2)}, u32[]{:S(2)}) collective-permute-start(f32[1,1,1,1,1,32,16]{5,6,4,3,2,1,0:T(8,128)S(1)} %fusion.62), channel_id=1, source_target_pairs={{0,4},{1,5},{2,6},{3,7},{4,0},{5,1},{6,2},{7,3},{8,12},{9,13},{10,... | collective-permute-start | bytes 6152 | tf_op jit(solution)/shard_map/ppermute | solution.py:135
  80.7 34.9 %collective-permute-start.17 = (bf16[1,2,1,2,2,32,2048]{6,5,4,3,2,1,0:T(8,128)(2,1)}, bf16[1,2,1,2,2,32,2048]{6,5,4,3,2,1,0:T(8,128)(2,1)}, u32[]{:S(2)}, u32[]{:S(2)}) collective-permute-start(bf16[1,2,1,2,2,32,2048]{6,5,4,3,2,1,0:T(8,128)(2,1)} %pad_maximum_fusion.5), channel_id=1, source_target_pairs={{0,2},{1,3},{2,0},{3,1},{4,6},{5,7},{6,4},{7,5},{8,10},{9,11},{10,... | collective-permute-start | bytes 3145736 | tf_op jit(solution)/shard_map/ppermute | solution.py:135
  82.4 5.0 %collective-permute-start.6 = (f32[1,1,1,1,2,32,16]{5,6,4,3,2,1,0:T(8,128)}, f32[1,1,1,1,2,32,16]{5,6,4,3,2,1,0:T(8,128)}, u32[]{:S(2)}, u32[]{:S(2)}) collective-permute-start(f32[1,1,1,1,2,32,16]{5,6,4,3,2,1,0:T(8,128)} %pad_maximum_fusion.13), channel_id=1, source_target_pairs={{0,8},{1,9},{2,10},{3,11},{4,12},{5,13},{6,14},{7,15},{8,0},{9,1},... | collective-permute-start | bytes 12296 | tf_op jit(solution)/shard_map/ppermute | solution.py:135
  88.1 16.9 %collective-permute-start.7 = (f32[1,1,1,2,2,32,16]{5,6,4,3,2,1,0:T(8,128)S(1)}, f32[1,1,1,2,2,32,16]{5,6,4,3,2,1,0:T(8,128)S(1)}, u32[]{:S(2)}, u32[]{:S(2)}) collective-permute-start(f32[1,1,1,2,2,32,16]{5,6,4,3,2,1,0:T(8,128)S(1)} %pad_maximum_fusion.12), channel_id=1, source_target_pairs={{0,2},{1,3},{2,0},{3,1},{4,6},{5,7},{6,4},{7,5},{8,10},{9,11},{10,... | collective-permute-start | bytes 24584 | tf_op jit(solution)/shard_map/ppermute | solution.py:135
  105.7 4.3 %collective-permute-start.8 = (f32[1,1,2,2,2,32,16]{5,6,4,3,2,1,0:T(8,128)S(1)}, f32[1,1,2,2,2,32,16]{5,6,4,3,2,1,0:T(8,128)S(1)}, u32[]{:S(2)}, u32[]{:S(2)}) collective-permute-start(f32[1,1,2,2,2,32,16]{5,6,4,3,2,1,0:T(8,128)S(1)} %pad_maximum_fusion.11), channel_id=1, source_target_pairs={{0,16},{16,0},{1,17},{17,1},{2,18},{18,2},{3,19},{19,3},{4,20},{20... | collective-permute-start | bytes 49160 | tf_op jit(solution)/shard_map/ppermute | solution.py:133
  111.3 1.7 collective-permute-start.9
  117.4 9.5 %collective-permute-start.18 = (bf16[1,2,2,2,2,32,2048]{6,5,4,3,2,1,0:T(8,128)(2,1)S(1)}, bf16[1,2,2,2,2,32,2048]{6,5,4,3,2,1,0:T(8,128)(2,1)S(1)}, u32[]{:S(2)}, u32[]{:S(2)}) collective-permute-start(bf16[1,2,2,2,2,32,2048]{6,5,4,3,2,1,0:T(8,128)(2,1)S(1)} %pad_maximum_fusion.3), channel_id=1, source_target_pairs={{0,1},{1,0},{2,3},{3,2},{4,5},{5,4},{6,7},{7,6},{8,9},{9,8},{10,11... | collective-permute-start | bytes 6291464 | tf_op jit(solution)/shard_map/ppermute | solution.py:135
  135.1 12.5 %collective-permute-start.23 = (f32[2,2,2,32,1]{3,4,2,1,0:T(1,128)S(1)}, f32[2,2,2,32,1]{3,4,2,1,0:T(1,128)S(1)}, u32[]{:S(2)}, u32[]{:S(2)}) collective-permute-start(f32[2,2,2,32,1]{3,4,2,1,0:T(1,128)S(1)} %squeeze.77), channel_id=1, source_target_pairs={{0,1},{1,0},{2,3},{3,2},{4,5},{5,4},{6,7},{7,6},{8,9},{9,8},{10,11... | collective-permute-start | bytes 3080 | tf_op jit(solution)/shard_map/ppermute | solution.py:135
  147.7 6.7 %collective-permute-start.24 = (f32[2,2,32,2]{2,3,1,0:T(2,128)S(1)}, f32[2,2,32,2]{2,3,1,0:T(2,128)S(1)}, u32[]{:S(2)}, u32[]{:S(2)}) collective-permute-start(f32[2,2,32,2]{2,3,1,0:T(2,128)S(1)} %get-tuple-element.25), channel_id=1, source_target_pairs={{0,2},{1,3},{2,0},{3,1},{4,6},{5,7},{6,4},{7,5},{8,10},{9,11},{10,... | collective-permute-start | bytes 3080 | tf_op jit(solution)/shard_map/ppermute | solution.py:135
  154.4 9.2 %copy-start.21 = (bf16[1024,768]{1,0:T(8,128)(2,1)S(1)}, bf16[1024,768]{1,0:T(8,128)(2,1)}, u32[]{:S(2)}) copy-start(bf16[1024,768]{1,0:T(8,128)(2,1)} %get-tuple-element.13) | copy-start | bytes 4718596
  154.4 4.6 %collective-permute-start.25 = (f32[2,32,4]{1,2,0:T(4,128)S(1)}, f32[2,32,4]{1,2,0:T(4,128)S(1)}, u32[]{:S(2)}, u32[]{:S(2)}) collective-permute-start(f32[2,32,4]{1,2,0:T(4,128)S(1)} %get-tuple-element.23), channel_id=1, source_target_pairs={{0,8},{1,9},{2,10},{3,11},{4,12},{5,13},{6,14},{7,15},{8,0},{9,1},... | collective-permute-start | bytes 3080 | tf_op jit(solution)/shard_map/ppermute | solution.py:135
  157.8 10.1 %collective-permute-start.10 = (bf16[2,2,2,32,2048]{4,3,2,1,0:T(8,128)(2,1)}, bf16[2,2,2,32,2048]{4,3,2,1,0:T(8,128)(2,1)}, u32[]{:S(2)}, u32[]{:S(2)}) collective-permute-start(bf16[2,2,2,32,2048]{4,3,2,1,0:T(8,128)(2,1)} %bitcast.9), channel_id=1, source_target_pairs={{0,1},{1,0},{2,3},{3,2},{4,5},{5,4},{6,7},{7,6},{8,9},{9,8},{10,11... | collective-permute-start | bytes 3145736 | tf_op jit(solution)/shard_map/ppermute | solution.py:135
  159.0 8.0 %copy-start.29 = (f32[32,16]{0,1:T(8,128)S(1)}, f32[32,16]{0,1:T(8,128)}, u32[]{:S(2)}) copy-start(f32[32,16]{0,1:T(8,128)} %copy-done.28) | copy-start | bytes 6148
  159.1 8.0 %copy-start.31 = (f32[32,16]{0,1:T(8,128)S(1)}, f32[32,16]{0,1:T(8,128)}, u32[]{:S(2)}) copy-start(f32[32,16]{0,1:T(8,128)} %copy-done.30) | copy-start | bytes 6148
  159.1 8.0 %copy-start.36 = (f32[32]{0:T(128)S(1)}, f32[32]{0:T(128)}, u32[]{:S(2)}) copy-start(f32[32]{0:T(128)} %copy-done.35) | copy-start | bytes 388
  159.1 7.8 %collective-permute-start.26 = (f32[32,8]{0,1:T(8,128)S(1)}, f32[32,8]{0,1:T(8,128)S(1)}, u32[]{:S(2)}, u32[]{:S(2)}) collective-permute-start(f32[32,8]{0,1:T(8,128)S(1)} %get-tuple-element.21), channel_id=1, source_target_pairs={{0,4},{1,5},{2,6},{3,7},{4,0},{5,1},{6,2},{7,3},{8,12},{9,13},{10,... | collective-permute-start | bytes 3080 | tf_op jit(solution)/shard_map/ppermute | solution.py:135
  166.7 4.2 %collective-permute-start.19 = (bf16[2,2,2,32,2048]{4,3,2,1,0:T(8,128)(2,1)}, bf16[2,2,2,32,2048]{4,3,2,1,0:T(8,128)(2,1)}, u32[]{:S(2)}, u32[]{:S(2)}) collective-permute-start(bf16[2,2,2,32,2048]{4,3,2,1,0:T(8,128)(2,1)} %bitcast.23), channel_id=1, source_target_pairs={{0,1},{1,0},{2,3},{3,2},{4,5},{5,4},{6,7},{7,6},{8,9},{9,8},{10,11... | collective-permute-start | bytes 3145736 | tf_op jit(solution)/shard_map/ppermute | solution.py:135
  170.1 15.0 %collective-permute-start.11 = (bf16[2,2,32,2048]{3,2,1,0:T(8,128)(2,1)S(1)}, bf16[2,2,32,2048]{3,2,1,0:T(8,128)(2,1)S(1)}, u32[]{:S(2)}, u32[]{:S(2)}) collective-permute-start(bf16[2,2,32,2048]{3,2,1,0:T(8,128)(2,1)S(1)} %slice_bitcast_fusion.2), channel_id=1, source_target_pairs={{0,2},{1,3},{2,0},{3,1},{4,6},{5,7},{6,4},{7,5},{8,10},{9,11},{10,... | collective-permute-start | bytes 1572872 | tf_op jit(solution)/shard_map/ppermute | solution.py:135
  172.5 42.8 %copy-start.27 = (bf16[2048,16]{0,1:T(8,128)(2,1)S(1)}, bf16[2048,16]{0,1:T(8,128)(2,1)}, u32[]{:S(2)}) copy-start(bf16[2048,16]{0,1:T(8,128)(2,1)} %param.11) | copy-start | bytes 196612
  172.5 23.2 %collective-permute-start.20 = (bf16[2,2,32,2048]{3,2,1,0:T(8,128)(2,1)S(1)}, bf16[2,2,32,2048]{3,2,1,0:T(8,128)(2,1)S(1)}, u32[]{:S(2)}, u32[]{:S(2)}) collective-permute-start(bf16[2,2,32,2048]{3,2,1,0:T(8,128)(2,1)S(1)} %slice_bitcast_fusion), channel_id=1, source_target_pairs={{0,2},{1,3},{2,0},{3,1},{4,6},{5,7},{6,4},{7,5},{8,10},{9,11},{10,... | collective-permute-start | bytes 1572872 | tf_op jit(solution)/shard_map/ppermute | solution.py:135
  185.3 17.2 %collective-permute-start.12 = (bf16[2,32,2048]{2,1,0:T(8,128)(2,1)S(1)}, bf16[2,32,2048]{2,1,0:T(8,128)(2,1)S(1)}, u32[]{:S(2)}, u32[]{:S(2)}) collective-permute-start(bf16[2,32,2048]{2,1,0:T(8,128)(2,1)S(1)} %slice_bitcast_fusion.6), channel_id=1, source_target_pairs={{0,8},{1,9},{2,10},{3,11},{4,12},{5,13},{6,14},{7,15},{8,0},{9,1},... | collective-permute-start | bytes 786440 | tf_op jit(solution)/shard_map/ppermute | solution.py:135
  195.9 13.8 %collective-permute-start.21 = (bf16[2,32,2048]{2,1,0:T(8,128)(2,1)S(1)}, bf16[2,32,2048]{2,1,0:T(8,128)(2,1)S(1)}, u32[]{:S(2)}, u32[]{:S(2)}) collective-permute-start(bf16[2,32,2048]{2,1,0:T(8,128)(2,1)S(1)} %slice_bitcast_fusion.4), channel_id=1, source_target_pairs={{0,8},{1,9},{2,10},{3,11},{4,12},{5,13},{6,14},{7,15},{8,0},{9,1},... | collective-permute-start | bytes 786440 | tf_op jit(solution)/shard_map/ppermute | solution.py:135
  202.6 9.8 %collective-permute-start.13 = (bf16[32,2048]{1,0:T(8,128)(2,1)S(1)}, bf16[32,2048]{1,0:T(8,128)(2,1)S(1)}, u32[]{:S(2)}, u32[]{:S(2)}) collective-permute-start(bf16[32,2048]{1,0:T(8,128)(2,1)S(1)} %slice_bitcast_fusion.10), channel_id=1, source_target_pairs={{0,4},{1,5},{2,6},{3,7},{4,0},{5,1},{6,2},{7,3},{8,12},{9,13},{10,... | collective-permute-start | bytes 393224 | tf_op jit(solution)/shard_map/ppermute | solution.py:135
  209.8 5.6 %collective-permute-start.22 = (bf16[32,2048]{1,0:T(8,128)(2,1)S(1)}, bf16[32,2048]{1,0:T(8,128)(2,1)S(1)}, u32[]{:S(2)}, u32[]{:S(2)}) collective-permute-start(bf16[32,2048]{1,0:T(8,128)(2,1)S(1)} %slice_bitcast_fusion.8), channel_id=1, source_target_pairs={{0,4},{1,5},{2,6},{3,7},{4,0},{5,1},{6,2},{7,3},{8,12},{9,13},{10,... | collective-permute-start | bytes 393224 | tf_op jit(solution)/shard_map/ppermute | solution.py:135
  (23 other events, 94.5 us)
Sparse Core Ops, SparseCore 0:
  168.1 131.0 all-reduce.1

commit v3 on v2

--- a/solution.py
+++ b/solution.py
@@ -240,7 +240,9 @@
     router_term = jnp.einsum(
         "td,te->de", tokens.astype(jnp.float32), logit_grad, precision=lax.Precision.HIGHEST
     )
-    router_grad = lax.psum(router_term, ("dp", "expert"))
+    router_grad = router_term
+    for bit in (1, 2, 0, 8, 4):
+        router_grad = router_grad + swap(router_grad, bit)
     router_back = jnp.einsum(
         "te,de->td", logit_grad, router_weight.astype(jnp.float32), precision=lax.Precision.HIGHEST
     )

time: 308 us -> 215 us (0.70)
  waiting for transfers between devices: 195 us -> 117 us
  between operations: 14.7 us -> 1.38 us
  starting transfers between devices: 31.6 us -> 41.4 us
  other arithmetic: 23.1 us -> 19 us
  local copies, waits for them, and re-layouts: 8.75 us -> 4.77 us
    psum x1 -> x0, waiting for transfers between devices: 82.8 us -> none  [local_dense(): router_grad = lax.psum(router_term, ('dp', 'expert'))]
    ppermute x24 -> x28, starting transfers between devices: 28.9 us -> 37.1 us  [swap(): return lax.ppermute(array, 'expert', [(i, i ^ bit) for i in range(size)])]
    ppermute x3 -> x4, waiting for transfers between devices: 12.6 us -> 15 us  [swap(): return lax.ppermute(array, 'dp', [(0, 1), (1, 0)])]
    ppermute x24 -> x28, waiting for transfers between devices: 99.8 us -> 102 us  [swap(): return lax.ppermute(array, 'expert', [(i, i ^ bit) for i in range(size)])]
  transfers between devices with their start and end apart: 28 -> 32, of which waited for: 19 -> 24; matrix products, arithmetic and copies ran while one was open for 17% -> 19% of each run, Pallas kernels for 0% -> 0%
where the time goes in v3:
time: 215 us
  waiting for transfers between devices  117 us (54%)
  starting transfers between devices  41.4 us (19%)
  matrix products  31.4 us (15%)
  other arithmetic  19 us (9%)
  local copies, waits for them, and re-layouts  4.77 us (2%)
    ppermute x28, waiting for transfers between devices, swap(): return lax.ppermute(array, 'expert', [(i, i ^ bit) for i in range(size)])  102 us
    ppermute x28, starting transfers between devices, swap(): return lax.ppermute(array, 'expert', [(i, i ^ bit) for i in range(size)])  37.1 us
    ppermute x4, waiting for transfers between devices, swap(): return lax.ppermute(array, 'dp', [(0, 1), (1, 0)])  15 us
    concatenate x14, other arithmetic, gather(): array = jnp.concatenate([array, swap(array, bit)], axis=bits.index(bit))  13.3 us
    dot_general x1, matrix products, local_dense(): lax.dot_general(cot_all, down_mat, (((1,), (1,)), ((), ())), preferred_el...  6.54 us
  transfers between devices with their start and end apart: 32, of which 24 were waited for; matrix products, arithmetic and copies ran while one was open for 19% of the time, Pallas kernels for 0%

profile of v3, /device:TPU:0, one launch (start us, length us, event | category | flops | bytes accessed | tf_op | source)
XLA Modules:
  0.0 214.7 jit_solution(8400251895410504167)
XLA Ops:
  0.7 3.1 %collective-permute-start = (bf16[1,1,1,1,1,32,2048]{6,5,4,3,2,1,0:T(8,128)(2,1)}, bf16[1,1,1,1,1,32,2048]{6,5,4,3,2,1,0:T(8,128)(2,1)S(1)}, u32[]{:S(2)}, u32[]{:S(2)}) collective-permute-start(bf16[1,1,1,1,1,32,2048]{6,5,4,3,2,1,0:T(8,128)(2,1)} %bitcast.114), channel_id=1, source_target_pairs={{0,4},{1,5},{2,6},{3,7},{4,0},{5,1},{6,2},{7,3},{8,12},{9,13},{10,... | collective-permute-start | bytes 393224 | tf_op jit(solution)/shard_map/ppermute | solution.py:135
  3.8 3.7 %collective-permute-done = bf16[1,1,1,1,1,32,2048]{6,5,4,3,2,1,0:T(8,128)(2,1)S(1)} collective-permute-done((bf16[1,1,1,1,1,32,2048]{6,5,4,3,2,1,0:T(8,128)(2,1)}, bf16[1,1,1,1,1,32,2048]{6,5,4,3,2,1,0:T(8,128)(2,1)S(1)}, u32[]{:S(2)}, u32[]{:S(2)}) %collective-permute-start) | collective-permute-done | bytes 131104 | tf_op jit(solution)/shard_map/ppermute | solution.py:135
  8.5 2.8 %collective-permute-start.1 = (bf16[1,1,1,1,2,32,2048]{6,5,4,3,2,1,0:T(8,128)(2,1)S(1)}, bf16[1,1,1,1,2,32,2048]{6,5,4,3,2,1,0:T(8,128)(2,1)S(1)}, u32[]{:S(2)}, u32[]{:S(2)}) collective-permute-start(bf16[1,1,1,1,2,32,2048]{6,5,4,3,2,1,0:T(8,128)(2,1)S(1)} %pad_maximum_fusion.8), channel_id=1, source_target_pairs={{0,8},{1,9},{2,10},{3,11},{4,12},{5,13},{6,14},{7,15},{8,0},{9,1},... | collective-permute-start | bytes 786440 | tf_op jit(solution)/shard_map/ppermute | solution.py:135
  11.3 11.3 %collective-permute-done.1 = bf16[1,1,1,1,2,32,2048]{6,5,4,3,2,1,0:T(8,128)(2,1)S(1)} collective-permute-done((bf16[1,1,1,1,2,32,2048]{6,5,4,3,2,1,0:T(8,128)(2,1)S(1)}, bf16[1,1,1,1,2,32,2048]{6,5,4,3,2,1,0:T(8,128)(2,1)S(1)}, u32[]{:S(2)}, u32[]{:S(2)}) %collective-permute-start.1) | collective-permute-done | bytes 262176 | tf_op jit(solution)/shard_map/ppermute | solution.py:135
  23.5 1.4 collective-permute-start.2
  24.9 11.6 %collective-permute-done.2 = bf16[1,1,1,2,2,32,2048]{6,5,4,3,2,1,0:T(8,128)(2,1)S(1)} collective-permute-done((bf16[1,1,1,2,2,32,2048]{6,5,4,3,2,1,0:T(8,128)(2,1)S(1)}, bf16[1,1,1,2,2,32,2048]{6,5,4,3,2,1,0:T(8,128)(2,1)S(1)}, u32[]{:S(2)}, u32[]{:S(2)}) %collective-permute-start.2) | collective-permute-done | bytes 524320 | tf_op jit(solution)/shard_map/ppermute | solution.py:135
  38.9 1.8 collective-permute-start.14
  40.7 3.2 %collective-permute-done.14 = bf16[1,1,1,1,1,32,2048]{6,5,4,3,2,1,0:T(8,128)(2,1)S(1)} collective-permute-done((bf16[1,1,1,1,1,32,2048]{6,5,4,3,2,1,0:T(8,128)(2,1)S(1)}, bf16[1,1,1,1,1,32,2048]{6,5,4,3,2,1,0:T(8,128)(2,1)S(1)}, u32[]{:S(2)}, u32[]{:S(2)}) %collective-permute-start.14) | collective-permute-done | bytes 131104 | tf_op jit(solution)/shard_map/ppermute | solution.py:135
  43.9 3.2 %collective-permute-start.15 = (bf16[1,1,1,1,2,32,2048]{6,5,4,3,2,1,0:T(8,128)(2,1)S(1)}, bf16[1,1,1,1,2,32,2048]{6,5,4,3,2,1,0:T(8,128)(2,1)S(1)}, u32[]{:S(2)}, u32[]{:S(2)}) collective-permute-start(bf16[1,1,1,1,2,32,2048]{6,5,4,3,2,1,0:T(8,128)(2,1)S(1)} %pad_maximum_fusion.9), channel_id=1, source_target_pairs={{0,8},{1,9},{2,10},{3,11},{4,12},{5,13},{6,14},{7,15},{8,0},{9,1},... | collective-permute-start | bytes 786440 | tf_op jit(solution)/shard_map/ppermute | solution.py:135
  47.1 10.4 %collective-permute-done.15 = bf16[1,1,1,1,2,32,2048]{6,5,4,3,2,1,0:T(8,128)(2,1)S(1)} collective-permute-done((bf16[1,1,1,1,2,32,2048]{6,5,4,3,2,1,0:T(8,128)(2,1)S(1)}, bf16[1,1,1,1,2,32,2048]{6,5,4,3,2,1,0:T(8,128)(2,1)S(1)}, u32[]{:S(2)}, u32[]{:S(2)}) %collective-permute-start.15) | collective-permute-done | bytes 262176 | tf_op jit(solution)/shard_map/ppermute | solution.py:135
  58.1 4.7 %collective-permute-done.3 = bf16[1,1,2,2,2,32,2048]{6,5,4,3,2,1,0:T(8,128)(2,1)S(1)} collective-permute-done((bf16[1,1,2,2,2,32,2048]{6,5,4,3,2,1,0:T(8,128)(2,1)S(1)}, bf16[1,1,2,2,2,32,2048]{6,5,4,3,2,1,0:T(8,128)(2,1)S(1)}, u32[]{:S(2)}, u32[]{:S(2)}) %collective-permute-start.3) | collective-permute-done | bytes 1048608 | tf_op jit(solution)/shard_map/ppermute | solution.py:133
  62.8 1.7 pad_maximum_fusion.2
  64.8 7.4 %collective-permute-done.16 = bf16[1,1,1,2,2,32,2048]{6,5,4,3,2,1,0:T(8,128)(2,1)S(1)} collective-permute-done((bf16[1,1,1,2,2,32,2048]{6,5,4,3,2,1,0:T(8,128)(2,1)S(1)}, bf16[1,1,1,2,2,32,2048]{6,5,4,3,2,1,0:T(8,128)(2,1)S(1)}, u32[]{:S(2)}, u32[]{:S(2)}) %collective-permute-start.16) | collective-permute-done | bytes 524320 | tf_op jit(solution)/shard_map/ppermute | solution.py:133
  75.2 2.9 %collective-permute-start.5 = (f32[1,1,1,1,1,32,16]{5,6,4,3,2,1,0:T(8,128)S(1)}, f32[1,1,1,1,1,32,16]{5,6,4,3,2,1,0:T(8,128)S(1)}, u32[]{:S(2)}, u32[]{:S(2)}) collective-permute-start(f32[1,1,1,1,1,32,16]{5,6,4,3,2,1,0:T(8,128)S(1)} %fusion.62), channel_id=1, source_target_pairs={{0,4},{1,5},{2,6},{3,7},{4,0},{5,1},{6,2},{7,3},{8,12},{9,13},{10,... | collective-permute-start | bytes 6152 | tf_op jit(solution)/shard_map/ppermute | solution.py:135
  78.1 1.6 collective-permute-done.5
  79.7 3.4 %collective-permute-start.6 = (f32[1,1,1,1,2,32,16]{5,6,4,3,2,1,0:T(8,128)S(1)}, f32[1,1,1,1,2,32,16]{5,6,4,3,2,1,0:T(8,128)S(1)}, u32[]{:S(2)}, u32[]{:S(2)}) collective-permute-start(f32[1,1,1,1,2,32,16]{5,6,4,3,2,1,0:T(8,128)S(1)} %pad_maximum_fusion.13), channel_id=1, source_target_pairs={{0,8},{1,9},{2,10},{3,11},{4,12},{5,13},{6,14},{7,15},{8,0},{9,1},... | collective-permute-start | bytes 12296 | tf_op jit(solution)/shard_map/ppermute | solution.py:135
  83.1 1.7 collective-permute-done.6
  86.6 11.9 %collective-permute-done.7 = f32[1,1,1,2,2,32,16]{5,6,4,3,2,1,0:T(8,128)} collective-permute-done((f32[1,1,1,2,2,32,16]{5,6,4,3,2,1,0:T(8,128)}, f32[1,1,1,2,2,32,16]{5,6,4,3,2,1,0:T(8,128)}, u32[]{:S(2)}, u32[]{:S(2)}) %collective-permute-start.7) | collective-permute-done | bytes 8224 | tf_op jit(solution)/shard_map/ppermute | solution.py:135
  101.3 2.2 %collective-permute-done.8 = f32[1,1,2,2,2,32,16]{5,6,4,3,2,1,0:T(8,128)S(1)} collective-permute-done((f32[1,1,2,2,2,32,16]{5,6,4,3,2,1,0:T(8,128)S(1)}, f32[1,1,2,2,2,32,16]{5,6,4,3,2,1,0:T(8,128)S(1)}, u32[]{:S(2)}, u32[]{:S(2)}) %collective-permute-start.8) | collective-permute-done | bytes 16416 | tf_op jit(solution)/shard_map/ppermute | solution.py:133
  105.7 1.5 fusion.48
  108.0 1.8 pad_maximum_fusion.3
  110.1 1.9 pad_maximum_fusion
  112.5 3.4 %fusion.10 = f32[1024,768]{1,0:T(8,128)S(1)} fusion(bf16[1024,2048]{1,0:T(8,128)(2,1)S(1)} %bitcast.120, bf16[1,2048,768]{2,1,0:T(8,128)(2,1)S(1)} %copy-done.39), kind=kOutput, calls=%fused_computation.13 | convolution fusion | flops 3221225472 | bytes 10485760 | tf_op jit(solution)/shard_map/dot_general | solution.py:173
  115.9 3.4 %fusion.6 = f32[1024,768]{1,0:T(8,128)S(1)} fusion(bf16[1024,2048]{1,0:T(8,128)(2,1)S(1)} %bitcast.121, bf16[1,2048,768]{2,1,0:T(8,128)(2,1)S(1)} %copy-done.38), kind=kOutput, calls=%fused_computation.9 | convolution fusion | flops 3221225472 | bytes 10485760 | tf_op jit(solution)/shard_map/dot_general | solution.py:174
  119.4 1.5 pad_maximum_fusion.1
  121.0 6.5 %multiply_reduce_fusion = (f32[1024]{0:T(1024)S(1)}, bf16[1024,768]{1,0:T(8,128)(2,1)}, bf16[1024,768]{1,0:T(8,128)(2,1)}, bf16[1024,768]{1,0:T(8,128)(2,1)}) fusion(f32[1024,768]{1,0:T(8,128)S(1)} %fusion.6, f32[1024,768]{1,0:T(8,128)S(1)} %fusion.10, f32[1024]{0:T(1024)S(1)} %mul.85, bf16[1024,2048]{1,0:T(8,128)(2,1)S(1)} %bitcast.124, ...), kind=kOutput, calls=%fused_computation.15 | convolution fusion | flops 3236166656 | bytes 18358272 | tf_op jit(solution)/shard_map/dot_general | solution.py:175
  129.2 1.6 collective-permute-start.24
  130.8 3.9 %fusion.4 = f32[512,2048]{1,0:T(8,128)S(1)} fusion(bf16[512,768]{1,0:T(8,128)(2,1)S(1)} %bitcast.138, bf16[1,2048,768]{2,1,0:T(8,128)(2,1)} %param.13), kind=kOutput, calls=%fused_computation.7 | convolution fusion | flops 1610612736 | bytes 8126464 | tf_op jit(solution)/shard_map/dot_general | solution.py:205
  134.8 1.9 add_convert_fusion
  136.7 2.5 %collective-permute-done.25 = f32[2,32,4]{1,2,0:T(4,128)S(1)} collective-permute-done((f32[2,32,4]{1,2,0:T(4,128)S(1)}, f32[2,32,4]{1,2,0:T(4,128)S(1)}, u32[]{:S(2)}, u32[]{:S(2)}) %collective-permute-start.25) | collective-permute-done | bytes 1056 | tf_op jit(solution)/shard_map/ppermute | solution.py:135
  139.3 3.3 %collective-permute-start.26 = (f32[32,8]{0,1:T(8,128)S(1)}, f32[32,8]{0,1:T(8,128)S(1)}, u32[]{:S(2)}, u32[]{:S(2)}) collective-permute-start(f32[32,8]{0,1:T(8,128)S(1)} %get-tuple-element.21), channel_id=1, source_target_pairs={{0,4},{1,5},{2,6},{3,7},{4,0},{5,1},{6,2},{7,3},{8,12},{9,13},{10,... | collective-permute-start | bytes 3080 | tf_op jit(solution)/shard_map/ppermute | solution.py:135
  144.7 1.8 fusion.13
  147.4 5.2 %collective-permute-done.28 = f32[2048,16]{0,1:T(8,128)S(1)} collective-permute-done((f32[2048,16]{0,1:T(8,128)S(1)}, f32[2048,16]{0,1:T(8,128)S(1)}, u32[]{:S(2)}, u32[]{:S(2)}) %collective-permute-start.28) | collective-permute-done | bytes 131104 | tf_op jit(solution)/shard_map/ppermute | solution.py:135
  152.6 1.6 collective-permute-start.29
  154.2 3.0 %fusion.35 = bf16[1,768,1024]{2,1,0:T(8,128)(2,1)} fusion(bf16[1024,768]{1,0:T(8,128)(2,1)S(1)} %copy-done.22, bf16[1024,2048]{1,0:T(8,128)(2,1)S(1)} %bitcast.125, s32[]{:T(128)S(6)} %select_n.4), kind=kOutput, calls=%fused_computation.38 | convolution fusion | flops 1611399168 | bytes 5242884 | tf_op jit(solution)/shard_map/dot_general | solution.py:223
  157.8 2.6 %collective-permute-start.30 = (f32[2048,16]{0,1:T(8,128)S(1)}, f32[2048,16]{0,1:T(8,128)S(1)}, u32[]{:S(2)}, u32[]{:S(2)}) collective-permute-start(f32[2048,16]{0,1:T(8,128)S(1)} %add.70), channel_id=1, source_target_pairs={{0,8},{1,9},{2,10},{3,11},{4,12},{5,13},{6,14},{7,15},{8,0},{9,1},... | collective-permute-start | bytes 393224 | tf_op jit(solution)/shard_map/ppermute | solution.py:135
  160.4 3.1 %fusion.38 = bf16[1,1024,768]{2,1,0:T(8,128)(2,1)} fusion(bf16[1024,768]{1,0:T(8,128)(2,1)S(1)} %copy-done.21, bf16[1024,2048]{1,0:T(8,128)(2,1)S(1)} %bitcast.122, s32[]{:T(128)S(6)} %select_n.4), kind=kOutput, calls=%fused_computation.39 | convolution fusion | flops 1611399168 | bytes 5242884 | tf_op jit(solution)/shard_map/dot_general | solution.py:220
  163.5 2.4 %collective-permute-done.30 = f32[2048,16]{0,1:T(8,128)S(1)} collective-permute-done((f32[2048,16]{0,1:T(8,128)S(1)}, f32[2048,16]{0,1:T(8,128)S(1)}, u32[]{:S(2)}, u32[]{:S(2)}) %collective-permute-start.30) | collective-permute-done | bytes 131104 | tf_op jit(solution)/shard_map/ppermute | solution.py:135
  166.5 3.1 %fusion.41 = bf16[1,1024,768]{2,1,0:T(8,128)(2,1)} fusion(bf16[1024,768]{1,0:T(8,128)(2,1)S(1)} %copy-done.20, bf16[1024,2048]{1,0:T(8,128)(2,1)S(1)} %bitcast.123, s32[]{:T(128)S(6)} %select_n.4), kind=kOutput, calls=%fused_computation.40 | convolution fusion | flops 1611399168 | bytes 5242884 | tf_op jit(solution)/shard_map/dot_general | solution.py:217
  169.6 1.4 collective-permute-done.31
  173.2 1.6 collective-permute-start.11
  174.7 12.3 %collective-permute-done.20 = bf16[2,2,32,2048]{3,2,1,0:T(8,128)(2,1)S(1)} collective-permute-done((bf16[2,2,32,2048]{3,2,1,0:T(8,128)(2,1)S(1)}, bf16[2,2,32,2048]{3,2,1,0:T(8,128)(2,1)S(1)}, u32[]{:S(2)}, u32[]{:S(2)}) %collective-permute-start.20) | collective-permute-done | bytes 524320 | tf_op jit(solution)/shard_map/ppermute | solution.py:135
  187.2 2.1 collective-permute-start.21
  189.3 5.9 %collective-permute-done.11 = bf16[2,2,32,2048]{3,2,1,0:T(8,128)(2,1)S(1)} collective-permute-done((bf16[2,2,32,2048]{3,2,1,0:T(8,128)(2,1)S(1)}, bf16[2,2,32,2048]{3,2,1,0:T(8,128)(2,1)S(1)}, u32[]{:S(2)}, u32[]{:S(2)}) %collective-permute-start.11) | collective-permute-done | bytes 524320 | tf_op jit(solution)/shard_map/ppermute | solution.py:135
  195.4 3.1 %collective-permute-start.12 = (bf16[2,32,2048]{2,1,0:T(8,128)(2,1)S(1)}, bf16[2,32,2048]{2,1,0:T(8,128)(2,1)S(1)}, u32[]{:S(2)}, u32[]{:S(2)}) collective-permute-start(bf16[2,32,2048]{2,1,0:T(8,128)(2,1)S(1)} %slice_bitcast_fusion.6), channel_id=1, source_target_pairs={{0,8},{1,9},{2,10},{3,11},{4,12},{5,13},{6,14},{7,15},{8,0},{9,1},... | collective-permute-start | bytes 786440 | tf_op jit(solution)/shard_map/ppermute | solution.py:135
  198.4 2.1 collective-permute-done.21
  200.7 8.0 %collective-permute-done.12 = bf16[2,32,2048]{2,1,0:T(8,128)(2,1)S(1)} collective-permute-done((bf16[2,32,2048]{2,1,0:T(8,128)(2,1)S(1)}, bf16[2,32,2048]{2,1,0:T(8,128)(2,1)S(1)}, u32[]{:S(2)}, u32[]{:S(2)}) %collective-permute-start.12) | collective-permute-done | bytes 262176 | tf_op jit(solution)/shard_map/ppermute | solution.py:135
  211.0 3.0 %collective-permute-done.13 = bf16[32,2048]{1,0:T(8,128)(2,1)S(1)} collective-permute-done((bf16[32,2048]{1,0:T(8,128)(2,1)S(1)}, bf16[32,2048]{1,0:T(8,128)(2,1)S(1)}, u32[]{:S(2)}, u32[]{:S(2)}) %collective-permute-start.13) | collective-permute-done | bytes 131104 | tf_op jit(solution)/shard_map/ppermute | solution.py:135
  (166 shorter events, 28.0 us)
Async XLA Ops:
  0.6 120.3 %copy-start = (bf16[1,768,2048]{2,1,0:T(8,128)(2,1)S(1)}, bf16[1,768,2048]{2,1,0:T(8,128)(2,1)}, u32[]{:S(2)}) copy-start(bf16[1,768,2048]{2,1,0:T(8,128)(2,1)} %param.14) | copy-start | bytes 9437188
  0.6 62.2 %copy-start.1 = (bf16[32,2048]{1,0:T(8,128)(2,1)S(1)}, bf16[32,2048]{1,0:T(8,128)(2,1)}, u32[]{:S(2)}) copy-start(bf16[32,2048]{1,0:T(8,128)(2,1)} %param.8) | copy-start | bytes 393220
  0.7 38.2 %copy-start.14 = (bf16[32,2048]{1,0:T(8,128)(2,1)S(1)}, bf16[32,2048]{1,0:T(8,128)(2,1)}, u32[]{:S(2)}) copy-start(bf16[32,2048]{1,0:T(8,128)(2,1)} %param.10) | copy-start | bytes 393220
  0.7 46.4 %copy-start.36 = (s32[32,8]{0,1:T(8,128)S(1)}, s32[32,8]{0,1:T(8,128)}, u32[]{:S(2)}) copy-start(s32[32,8]{0,1:T(8,128)} %param.9) | copy-start | bytes 3076
  0.7 6.8 %collective-permute-start = (bf16[1,1,1,1,1,32,2048]{6,5,4,3,2,1,0:T(8,128)(2,1)}, bf16[1,1,1,1,1,32,2048]{6,5,4,3,2,1,0:T(8,128)(2,1)S(1)}, u32[]{:S(2)}, u32[]{:S(2)}) collective-permute-start(bf16[1,1,1,1,1,32,2048]{6,5,4,3,2,1,0:T(8,128)(2,1)} %bitcast.114), channel_id=1, source_target_pairs={{0,4},{1,5},{2,6},{3,7},{4,0},{5,1},{6,2},{7,3},{8,12},{9,13},{10,... | collective-permute-start | bytes 393224 | tf_op jit(solution)/shard_map/ppermute | solution.py:135
  7.5 57.0 %copy-start.16 = (bf16[1,1,1,1,1,32,2048]{6,5,4,3,2,1,0:T(8,128)(2,1)}, bf16[1,1,1,1,1,32,2048]{6,5,4,3,2,1,0:T(8,128)(2,1)S(1)}, u32[]{:S(2)}) copy-start(bf16[1,1,1,1,1,32,2048]{6,5,4,3,2,1,0:T(8,128)(2,1)S(1)} %collective-permute-done) | copy-start | bytes 393220
  8.5 14.1 %collective-permute-start.1 = (bf16[1,1,1,1,2,32,2048]{6,5,4,3,2,1,0:T(8,128)(2,1)S(1)}, bf16[1,1,1,1,2,32,2048]{6,5,4,3,2,1,0:T(8,128)(2,1)S(1)}, u32[]{:S(2)}, u32[]{:S(2)}) collective-permute-start(bf16[1,1,1,1,2,32,2048]{6,5,4,3,2,1,0:T(8,128)(2,1)S(1)} %pad_maximum_fusion.8), channel_id=1, source_target_pairs={{0,8},{1,9},{2,10},{3,11},{4,12},{5,13},{6,14},{7,15},{8,0},{9,1},... | collective-permute-start | bytes 786440 | tf_op jit(solution)/shard_map/ppermute | solution.py:135
  23.5 13.0 %collective-permute-start.2 = (bf16[1,1,1,2,2,32,2048]{6,5,4,3,2,1,0:T(8,128)(2,1)S(1)}, bf16[1,1,1,2,2,32,2048]{6,5,4,3,2,1,0:T(8,128)(2,1)S(1)}, u32[]{:S(2)}, u32[]{:S(2)}) collective-permute-start(bf16[1,1,1,2,2,32,2048]{6,5,4,3,2,1,0:T(8,128)(2,1)S(1)} %pad_maximum_fusion.6), channel_id=1, source_target_pairs={{0,2},{1,3},{2,0},{3,1},{4,6},{5,7},{6,4},{7,5},{8,10},{9,11},{10,... | collective-permute-start | bytes 1572872 | tf_op jit(solution)/shard_map/ppermute | solution.py:135
  36.5 28.0 %copy-start.2 = (bf16[1,1,1,2,2,32,2048]{6,5,4,3,2,1,0:T(8,128)(2,1)}, bf16[1,1,1,2,2,32,2048]{6,5,4,3,2,1,0:T(8,128)(2,1)S(1)}, u32[]{:S(2)}) copy-start(bf16[1,1,1,2,2,32,2048]{6,5,4,3,2,1,0:T(8,128)(2,1)S(1)} %collective-permute-done.2) | copy-start | bytes 1572868
  37.6 26.9 %copy-start.24 = (bf16[2048,16]{0,1:T(8,128)(2,1)S(1)}, bf16[2048,16]{0,1:T(8,128)(2,1)}, u32[]{:S(2)}) copy-start(bf16[2048,16]{0,1:T(8,128)(2,1)} %param.11) | copy-start | bytes 196612
  37.6 25.2 %collective-permute-start.3 = (bf16[1,1,2,2,2,32,2048]{6,5,4,3,2,1,0:T(8,128)(2,1)S(1)}, bf16[1,1,2,2,2,32,2048]{6,5,4,3,2,1,0:T(8,128)(2,1)S(1)}, u32[]{:S(2)}, u32[]{:S(2)}) collective-permute-start(bf16[1,1,2,2,2,32,2048]{6,5,4,3,2,1,0:T(8,128)(2,1)S(1)} %pad_maximum_fusion.4), channel_id=1, source_target_pairs={{0,16},{16,0},{1,17},{17,1},{2,18},{18,2},{3,19},{19,3},{4,20},{20... | collective-permute-start | bytes 3145736 | tf_op jit(solution)/shard_map/ppermute | solution.py:133
  38.9 5.0 %collective-permute-start.14 = (bf16[1,1,1,1,1,32,2048]{6,5,4,3,2,1,0:T(8,128)(2,1)S(1)}, bf16[1,1,1,1,1,32,2048]{6,5,4,3,2,1,0:T(8,128)(2,1)S(1)}, u32[]{:S(2)}, u32[]{:S(2)}) collective-permute-start(bf16[1,1,1,1,1,32,2048]{6,5,4,3,2,1,0:T(8,128)(2,1)S(1)} %bitcast.129), channel_id=1, source_target_pairs={{0,4},{1,5},{2,6},{3,7},{4,0},{5,1},{6,2},{7,3},{8,12},{9,13},{10,... | collective-permute-start | bytes 393224 | tf_op jit(solution)/shard_map/ppermute | solution.py:135
  43.9 30.2 %copy-start.18 = (bf16[1,1,1,1,1,32,2048]{6,5,4,3,2,1,0:T(8,128)(2,1)}, bf16[1,1,1,1,1,32,2048]{6,5,4,3,2,1,0:T(8,128)(2,1)S(1)}, u32[]{:S(2)}) copy-start(bf16[1,1,1,1,1,32,2048]{6,5,4,3,2,1,0:T(8,128)(2,1)S(1)} %collective-permute-done.14) | copy-start | bytes 393220
  43.9 13.6 %collective-permute-start.15 = (bf16[1,1,1,1,2,32,2048]{6,5,4,3,2,1,0:T(8,128)(2,1)S(1)}, bf16[1,1,1,1,2,32,2048]{6,5,4,3,2,1,0:T(8,128)(2,1)S(1)}, u32[]{:S(2)}, u32[]{:S(2)}) collective-permute-start(bf16[1,1,1,1,2,32,2048]{6,5,4,3,2,1,0:T(8,128)(2,1)S(1)} %pad_maximum_fusion.9), channel_id=1, source_target_pairs={{0,8},{1,9},{2,10},{3,11},{4,12},{5,13},{6,14},{7,15},{8,0},{9,1},... | collective-permute-start | bytes 786440 | tf_op jit(solution)/shard_map/ppermute | solution.py:135
  47.1 27.0 %copy-start.28 = (f32[32,16]{0,1:T(8,128)}, f32[32,16]{0,1:T(8,128)S(1)}, u32[]{:S(2)}) copy-start(f32[32,16]{0,1:T(8,128)S(1)} %convert_reduce_fusion) | copy-start | bytes 6148
  57.5 16.6 %copy-start.10 = (bf16[1,1,1,1,2,32,2048]{6,5,4,3,2,1,0:T(8,128)(2,1)}, bf16[1,1,1,1,2,32,2048]{6,5,4,3,2,1,0:T(8,128)(2,1)S(1)}, u32[]{:S(2)}) copy-start(bf16[1,1,1,1,2,32,2048]{6,5,4,3,2,1,0:T(8,128)(2,1)S(1)} %collective-permute-done.15) | copy-start | bytes 786436
  57.5 14.6 %collective-permute-start.16 = (bf16[1,1,1,2,2,32,2048]{6,5,4,3,2,1,0:T(8,128)(2,1)S(1)}, bf16[1,1,1,2,2,32,2048]{6,5,4,3,2,1,0:T(8,128)(2,1)S(1)}, u32[]{:S(2)}, u32[]{:S(2)}) collective-permute-start(bf16[1,1,1,2,2,32,2048]{6,5,4,3,2,1,0:T(8,128)(2,1)S(1)} %pad_maximum_fusion.7), channel_id=1, source_target_pairs={{0,16},{16,0},{1,17},{17,1},{2,18},{18,2},{3,19},{19,3},{4,20},{20... | collective-permute-start | bytes 1572872 | tf_op jit(solution)/shard_map/ppermute | solution.py:133
  62.8 11.2 %copy-start.12 = (bf16[1,1,2,2,2,32,2048]{6,5,4,3,2,1,0:T(8,128)(2,1)}, bf16[1,1,2,2,2,32,2048]{6,5,4,3,2,1,0:T(8,128)(2,1)S(1)}, u32[]{:S(2)}) copy-start(bf16[1,1,2,2,2,32,2048]{6,5,4,3,2,1,0:T(8,128)(2,1)S(1)} %collective-permute-done.3) | copy-start | bytes 3145732
  64.5 45.6 %collective-permute-start.4 = (bf16[1,2,2,2,2,32,2048]{6,5,4,3,2,1,0:T(8,128)(2,1)}, bf16[1,2,2,2,2,32,2048]{6,5,4,3,2,1,0:T(8,128)(2,1)}, u32[]{:S(2)}, u32[]{:S(2)}) collective-permute-start(bf16[1,2,2,2,2,32,2048]{6,5,4,3,2,1,0:T(8,128)(2,1)} %pad_maximum_fusion.2), channel_id=1, source_target_pairs={{0,1},{1,0},{2,3},{3,2},{4,5},{5,4},{6,7},{7,6},{8,9},{9,8},{10,11... | collective-permute-start | bytes 6291464 | tf_op jit(solution)/shard_map/ppermute | solution.py:135
  64.7 13.4 %copy-start.32 = (f32[32]{0:T(128)}, f32[32]{0:T(128)S(1)}, u32[]{:S(2)}) copy-start(f32[32]{0:T(128)S(1)} %get-tuple-element.26) | copy-start | bytes 388
  64.7 21.3 %copy-start.26 = (f32[32,16]{0,1:T(8,128)}, f32[32,16]{0,1:T(8,128)S(1)}, u32[]{:S(2)}) copy-start(f32[32,16]{0,1:T(8,128)S(1)} %get-tuple-element.27) | copy-start | bytes 6148
  64.7 21.8 %copy-start.30 = (f32[32,16]{0,1:T(8,128)}, f32[32,16]{0,1:T(8,128)S(1)}, u32[]{:S(2)}) copy-start(f32[32,16]{0,1:T(8,128)S(1)} %get-tuple-element.11) | copy-start | bytes 6148
  64.8 21.8 %copy-start.34 = (f32[32]{0:T(128)}, f32[32]{0:T(128)S(1)}, u32[]{:S(2)}) copy-start(f32[32]{0:T(128)S(1)} %get-tuple-element.10) | copy-start | bytes 388
  74.1 34.0 %collective-permute-start.17 = (bf16[1,2,1,2,2,32,2048]{6,5,4,3,2,1,0:T(8,128)(2,1)}, bf16[1,2,1,2,2,32,2048]{6,5,4,3,2,1,0:T(8,128)(2,1)}, u32[]{:S(2)}, u32[]{:S(2)}) collective-permute-start(bf16[1,2,1,2,2,32,2048]{6,5,4,3,2,1,0:T(8,128)(2,1)} %pad_maximum_fusion.5), channel_id=1, source_target_pairs={{0,2},{1,3},{2,0},{3,1},{4,6},{5,7},{6,4},{7,5},{8,10},{9,11},{10,... | collective-permute-start | bytes 3145736 | tf_op jit(solution)/shard_map/ppermute | solution.py:135
  75.2 4.5 %collective-permute-start.5 = (f32[1,1,1,1,1,32,16]{5,6,4,3,2,1,0:T(8,128)S(1)}, f32[1,1,1,1,1,32,16]{5,6,4,3,2,1,0:T(8,128)S(1)}, u32[]{:S(2)}, u32[]{:S(2)}) collective-permute-start(f32[1,1,1,1,1,32,16]{5,6,4,3,2,1,0:T(8,128)S(1)} %fusion.62), channel_id=1, source_target_pairs={{0,4},{1,5},{2,6},{3,7},{4,0},{5,1},{6,2},{7,3},{8,12},{9,13},{10,... | collective-permute-start | bytes 6152 | tf_op jit(solution)/shard_map/ppermute | solution.py:135
  79.7 5.1 %collective-permute-start.6 = (f32[1,1,1,1,2,32,16]{5,6,4,3,2,1,0:T(8,128)S(1)}, f32[1,1,1,1,2,32,16]{5,6,4,3,2,1,0:T(8,128)S(1)}, u32[]{:S(2)}, u32[]{:S(2)}) collective-permute-start(f32[1,1,1,1,2,32,16]{5,6,4,3,2,1,0:T(8,128)S(1)} %pad_maximum_fusion.13), channel_id=1, source_target_pairs={{0,8},{1,9},{2,10},{3,11},{4,12},{5,13},{6,14},{7,15},{8,0},{9,1},... | collective-permute-start | bytes 12296 | tf_op jit(solution)/shard_map/ppermute | solution.py:135
  86.0 12.4 %collective-permute-start.7 = (f32[1,1,1,2,2,32,16]{5,6,4,3,2,1,0:T(8,128)}, f32[1,1,1,2,2,32,16]{5,6,4,3,2,1,0:T(8,128)}, u32[]{:S(2)}, u32[]{:S(2)}) collective-permute-start(f32[1,1,1,2,2,32,16]{5,6,4,3,2,1,0:T(8,128)} %pad_maximum_fusion.12), channel_id=1, source_target_pairs={{0,2},{1,3},{2,0},{3,1},{4,6},{5,7},{6,4},{7,5},{8,10},{9,11},{10,... | collective-permute-start | bytes 24584 | tf_op jit(solution)/shard_map/ppermute | solution.py:135
  99.2 4.3 %collective-permute-start.8 = (f32[1,1,2,2,2,32,16]{5,6,4,3,2,1,0:T(8,128)S(1)}, f32[1,1,2,2,2,32,16]{5,6,4,3,2,1,0:T(8,128)S(1)}, u32[]{:S(2)}, u32[]{:S(2)}) collective-permute-start(f32[1,1,2,2,2,32,16]{5,6,4,3,2,1,0:T(8,128)S(1)} %pad_maximum_fusion.11), channel_id=1, source_target_pairs={{0,16},{16,0},{1,17},{17,1},{2,18},{18,2},{3,19},{19,3},{4,20},{20... | collective-permute-start | bytes 49160 | tf_op jit(solution)/shard_map/ppermute | solution.py:133
  104.3 1.4 collective-permute-start.9
  109.9 9.5 %collective-permute-start.18 = (bf16[1,2,2,2,2,32,2048]{6,5,4,3,2,1,0:T(8,128)(2,1)S(1)}, bf16[1,2,2,2,2,32,2048]{6,5,4,3,2,1,0:T(8,128)(2,1)S(1)}, u32[]{:S(2)}, u32[]{:S(2)}) collective-permute-start(bf16[1,2,2,2,2,32,2048]{6,5,4,3,2,1,0:T(8,128)(2,1)S(1)} %pad_maximum_fusion.3), channel_id=1, source_target_pairs={{0,1},{1,0},{2,3},{3,2},{4,5},{5,4},{6,7},{7,6},{8,9},{9,8},{10,11... | collective-permute-start | bytes 6291464 | tf_op jit(solution)/shard_map/ppermute | solution.py:135
  127.6 1.5 collective-permute-start.23
  129.2 5.5 %collective-permute-start.24 = (f32[2,2,32,2]{2,3,1,0:T(2,128)S(1)}, f32[2,2,32,2]{2,3,1,0:T(2,128)S(1)}, u32[]{:S(2)}, u32[]{:S(2)}) collective-permute-start(f32[2,2,32,2]{2,3,1,0:T(2,128)S(1)} %get-tuple-element.25), channel_id=1, source_target_pairs={{0,2},{1,3},{2,0},{3,1},{4,6},{5,7},{6,4},{7,5},{8,10},{9,11},{10,... | collective-permute-start | bytes 3080 | tf_op jit(solution)/shard_map/ppermute | solution.py:135
  134.7 4.6 %collective-permute-start.25 = (f32[2,32,4]{1,2,0:T(4,128)S(1)}, f32[2,32,4]{1,2,0:T(4,128)S(1)}, u32[]{:S(2)}, u32[]{:S(2)}) collective-permute-start(f32[2,32,4]{1,2,0:T(4,128)S(1)} %get-tuple-element.23), channel_id=1, source_target_pairs={{0,8},{1,9},{2,10},{3,11},{4,12},{5,13},{6,14},{7,15},{8,0},{9,1},... | collective-permute-start | bytes 3080 | tf_op jit(solution)/shard_map/ppermute | solution.py:135
  139.3 4.9 %collective-permute-start.26 = (f32[32,8]{0,1:T(8,128)S(1)}, f32[32,8]{0,1:T(8,128)S(1)}, u32[]{:S(2)}, u32[]{:S(2)}) collective-permute-start(f32[32,8]{0,1:T(8,128)S(1)} %get-tuple-element.21), channel_id=1, source_target_pairs={{0,4},{1,5},{2,6},{3,7},{4,0},{5,1},{6,2},{7,3},{8,12},{9,13},{10,... | collective-permute-start | bytes 3080 | tf_op jit(solution)/shard_map/ppermute | solution.py:135
  142.8 28.8 %collective-permute-start.19 = (bf16[2,2,2,32,2048]{4,3,2,1,0:T(8,128)(2,1)S(1)}, bf16[2,2,2,32,2048]{4,3,2,1,0:T(8,128)(2,1)S(1)}, u32[]{:S(2)}, u32[]{:S(2)}) collective-permute-start(bf16[2,2,2,32,2048]{4,3,2,1,0:T(8,128)(2,1)S(1)} %bitcast.134), channel_id=1, source_target_pairs={{0,1},{1,0},{2,3},{3,2},{4,5},{5,4},{6,7},{7,6},{8,9},{9,8},{10,11... | collective-permute-start | bytes 3145736 | tf_op jit(solution)/shard_map/ppermute | solution.py:135
  144.7 1.9 collective-permute-start.27
  146.6 6.0 %collective-permute-start.28 = (f32[2048,16]{0,1:T(8,128)S(1)}, f32[2048,16]{0,1:T(8,128)S(1)}, u32[]{:S(2)}, u32[]{:S(2)}) collective-permute-start(f32[2048,16]{0,1:T(8,128)S(1)} %add.68), channel_id=1, source_target_pairs={{0,2},{1,3},{2,0},{3,1},{4,6},{5,7},{6,4},{7,5},{8,10},{9,11},{10,... | collective-permute-start | bytes 393224 | tf_op jit(solution)/shard_map/ppermute | solution.py:135
  152.6 5.2 %collective-permute-start.29 = (f32[2048,16]{0,1:T(8,128)S(1)}, f32[2048,16]{0,1:T(8,128)S(1)}, u32[]{:S(2)}, u32[]{:S(2)}) collective-permute-start(f32[2048,16]{0,1:T(8,128)S(1)} %add.69), channel_id=1, source_target_pairs={{0,16},{16,0},{1,17},{17,1},{2,18},{18,2},{3,19},{19,3},{4,20},{20... | collective-permute-start | bytes 393224 | tf_op jit(solution)/shard_map/ppermute | solution.py:133
  157.8 8.1 %collective-permute-start.30 = (f32[2048,16]{0,1:T(8,128)S(1)}, f32[2048,16]{0,1:T(8,128)S(1)}, u32[]{:S(2)}, u32[]{:S(2)}) collective-permute-start(f32[2048,16]{0,1:T(8,128)S(1)} %add.70), channel_id=1, source_target_pairs={{0,8},{1,9},{2,10},{3,11},{4,12},{5,13},{6,14},{7,15},{8,0},{9,1},... | collective-permute-start | bytes 393224 | tf_op jit(solution)/shard_map/ppermute | solution.py:135
  163.5 9.2 %collective-permute-start.10 = (bf16[2,2,2,32,2048]{4,3,2,1,0:T(8,128)(2,1)S(1)}, bf16[2,2,2,32,2048]{4,3,2,1,0:T(8,128)(2,1)S(1)}, u32[]{:S(2)}, u32[]{:S(2)}) collective-permute-start(bf16[2,2,2,32,2048]{4,3,2,1,0:T(8,128)(2,1)S(1)} %bitcast.135), channel_id=1, source_target_pairs={{0,1},{1,0},{2,3},{3,2},{4,5},{5,4},{6,7},{7,6},{8,9},{9,8},{10,11... | collective-permute-start | bytes 3145736 | tf_op jit(solution)/shard_map/ppermute | solution.py:135
  165.9 5.0 %collective-permute-start.31 = (f32[2048,16]{0,1:T(8,128)S(1)}, f32[2048,16]{0,1:T(8,128)S(1)}, u32[]{:S(2)}, u32[]{:S(2)}) collective-permute-start(f32[2048,16]{0,1:T(8,128)S(1)} %add.71), channel_id=1, source_target_pairs={{0,4},{1,5},{2,6},{3,7},{4,0},{5,1},{6,2},{7,3},{8,12},{9,13},{10,... | collective-permute-start | bytes 393224 | tf_op jit(solution)/shard_map/ppermute | solution.py:135
  172.1 14.9 %collective-permute-start.20 = (bf16[2,2,32,2048]{3,2,1,0:T(8,128)(2,1)S(1)}, bf16[2,2,32,2048]{3,2,1,0:T(8,128)(2,1)S(1)}, u32[]{:S(2)}, u32[]{:S(2)}) collective-permute-start(bf16[2,2,32,2048]{3,2,1,0:T(8,128)(2,1)S(1)} %slice_bitcast_fusion), channel_id=1, source_target_pairs={{0,2},{1,3},{2,0},{3,1},{4,6},{5,7},{6,4},{7,5},{8,10},{9,11},{10,... | collective-permute-start | bytes 1572872 | tf_op jit(solution)/shard_map/ppermute | solution.py:135
  173.2 36.8 %copy-start.25 = (bf16[2048,16]{0,1:T(8,128)(2,1)S(1)}, bf16[2048,16]{0,1:T(8,128)(2,1)}, u32[]{:S(2)}) copy-start(bf16[2048,16]{0,1:T(8,128)(2,1)} %param.11) | copy-start | bytes 196612
  173.2 22.0 %collective-permute-start.11 = (bf16[2,2,32,2048]{3,2,1,0:T(8,128)(2,1)S(1)}, bf16[2,2,32,2048]{3,2,1,0:T(8,128)(2,1)S(1)}, u32[]{:S(2)}, u32[]{:S(2)}) collective-permute-start(bf16[2,2,32,2048]{3,2,1,0:T(8,128)(2,1)S(1)} %slice_bitcast_fusion.2), channel_id=1, source_target_pairs={{0,2},{1,3},{2,0},{3,1},{4,6},{5,7},{6,4},{7,5},{8,10},{9,11},{10,... | collective-permute-start | bytes 1572872 | tf_op jit(solution)/shard_map/ppermute | solution.py:135
  187.2 13.3 %collective-permute-start.21 = (bf16[2,32,2048]{2,1,0:T(8,128)(2,1)S(1)}, bf16[2,32,2048]{2,1,0:T(8,128)(2,1)S(1)}, u32[]{:S(2)}, u32[]{:S(2)}) collective-permute-start(bf16[2,32,2048]{2,1,0:T(8,128)(2,1)S(1)} %slice_bitcast_fusion.4), channel_id=1, source_target_pairs={{0,8},{1,9},{2,10},{3,11},{4,12},{5,13},{6,14},{7,15},{8,0},{9,1},... | collective-permute-start | bytes 786440 | tf_op jit(solution)/shard_map/ppermute | solution.py:135
  195.4 13.3 %collective-permute-start.12 = (bf16[2,32,2048]{2,1,0:T(8,128)(2,1)S(1)}, bf16[2,32,2048]{2,1,0:T(8,128)(2,1)S(1)}, u32[]{:S(2)}, u32[]{:S(2)}) collective-permute-start(bf16[2,32,2048]{2,1,0:T(8,128)(2,1)S(1)} %slice_bitcast_fusion.6), channel_id=1, source_target_pairs={{0,8},{1,9},{2,10},{3,11},{4,12},{5,13},{6,14},{7,15},{8,0},{9,1},... | collective-permute-start | bytes 786440 | tf_op jit(solution)/shard_map/ppermute | solution.py:135
  200.6 9.4 %collective-permute-start.22 = (bf16[32,2048]{1,0:T(8,128)(2,1)S(1)}, bf16[32,2048]{1,0:T(8,128)(2,1)S(1)}, u32[]{:S(2)}, u32[]{:S(2)}) collective-permute-start(bf16[32,2048]{1,0:T(8,128)(2,1)S(1)} %slice_bitcast_fusion.8), channel_id=1, source_target_pairs={{0,4},{1,5},{2,6},{3,7},{4,0},{5,1},{6,2},{7,3},{8,12},{9,13},{10,... | collective-permute-start | bytes 393224 | tf_op jit(solution)/shard_map/ppermute | solution.py:135
  208.8 5.2 %collective-permute-start.13 = (bf16[32,2048]{1,0:T(8,128)(2,1)S(1)}, bf16[32,2048]{1,0:T(8,128)(2,1)S(1)}, u32[]{:S(2)}, u32[]{:S(2)}) collective-permute-start(bf16[32,2048]{1,0:T(8,128)(2,1)S(1)} %slice_bitcast_fusion.10), channel_id=1, source_target_pairs={{0,4},{1,5},{2,6},{3,7},{4,0},{5,1},{6,2},{7,3},{8,12},{9,13},{10,... | collective-permute-start | bytes 393224 | tf_op jit(solution)/shard_map/ppermute | solution.py:135
  (25 other events, 120.6 us)
